TPU v7x, 32 devices: a whole 2x2x4 slice. The times are simulated.
32 devices in a mesh: seq: 16 (over z, y, x), tensor: 2 (over core).
Axes of the slice: x: 2, y: 2, z: 4, core: 2. Of those that a mesh axis runs over, the one named last changes fastest.
Arguments:
- residual: bfloat16 [2048, 2048], P('seq', 'tensor'), may hold values from -10 to 10
- queries: bfloat16 [2048, 2048], P('seq', 'tensor'), may hold values from -5 to 5
- new_keys: bfloat16 [2048, 2048], P('seq', 'tensor'), may hold values from -5 to 5
- new_values: bfloat16 [2048, 2048], P('seq', 'tensor'), may hold values from -6 to 6
- cache_keys: bfloat16 [4, 8192, 2048], P(None, 'seq', 'tensor'), may hold values from -5 to 5
- cache_values: bfloat16 [4, 8192, 2048], P(None, 'seq', 'tensor'), may hold values from -6 to 6
- cache_lengths: int32 [4], replicated, may hold values from 1 to 8192, 9728 in all
- out_proj: bfloat16 [2048, 2048], P('tensor'), may hold values from -0.125 to 0.125
- norm_gain: float32 [2048], P('tensor'), may hold values from 0.5 to 1.5
- router: bfloat16 [2048, 32], P('tensor'), may hold values from -0.3984375 to 0.3984375
- expert_ids: int32 [2048, 6], P('seq'), may hold values from 0 to 31, all different within a row; in each aligned block of 128 rows (0 to 127, 128 to 255, ...) at most 32 rows name the same one
- expert_gate_up: bfloat16 [32, 2048, 2, 1408], P('seq', None, None, 'tensor'), may hold values from -0.125 to 0.125
- expert_down: bfloat16 [32, 1408, 2048], P('seq', 'tensor'), may hold values from -0.15625 to 0.15625
- shared_gate_up: bfloat16 [2048, 2, 1408], P(None, None, 'tensor'), may hold values from -0.125 to 0.125
- shared_down: bfloat16 [1408, 2048], P('tensor'), may hold values from -0.15625 to 0.15625
Outputs:
- layer_out: bfloat16 [2048, 2048], P('seq', 'tensor')
Inputs may be any that keep to these rules, and one draw needn't show every extreme that they name: Request r's cached tokens are positions 0 to cache_lengths[r] - 1 of its row of 8192 cache positions; the lengths sum to 8192 + 3 * (512) and the longest equals 8192. `expert_ids`: each row names 6 different experts. Among the 128 rows of one index of seq no expert is named by more than 32 rows, and this bound is reached.
All inputs are finite; a program needn't handle non-finite values.
Results may differ from a plain program's by a relative error of at most 0.025.
Values may be sent and summed in bfloat16 or wider, within the bound.
A program may use at most 128 MiB of HBM per device.

v0:
```python
import math

import jax
import jax.numpy as jnp
from jax import lax
from jax.sharding import PartitionSpec as P

D = 2048
HD = 128
NEW = 512


negative = -1e30
epsilon = 1e-06


def block_partial(scores, visible, values):
    masked = jnp.where(visible, scores, negative)
    block_max = jnp.max(masked, -1)
    shifted = jnp.where(visible, scores, block_max[..., None]) - block_max[..., None]
    weights = jnp.where(visible, jnp.exp(shifted), 0.0)
    block_sum = jnp.sum(weights, -1)
    block_out = jnp.einsum(
        "hqk,khd->qhd", weights.astype(jnp.bfloat16), values, preferred_element_type=jnp.float32
    )
    return (block_max, block_sum, block_out)


def shards(
    residual,
    queries,
    new_keys,
    new_values,
    cache_keys,
    cache_values,
    cache_lengths,
    out_proj,
    norm_gain,
    router,
    expert_ids,
    expert_gate_up,
    expert_down,
    shared_gate_up,
    shared_down,
):
    seq_count = lax.axis_size("seq")
    tensor_count = lax.axis_size("tensor")
    seq_index = lax.axis_index("seq")
    tok_dev = queries.shape[0]
    heads_local = queries.shape[1] // HD
    requests = tok_dev * seq_count // NEW
    clen_dev = cache_keys.shape[1]
    tokens = tok_dev * seq_count
    width_local = residual.shape[1]
    experts = router.shape[1]
    exp_dev = expert_gate_up.shape[0]
    topk = expert_ids.shape[1]
    scaling = 1.0 / math.sqrt(HD)
    every_query = lax.all_gather(queries, "seq", axis=0, tiled=True)
    grouped = every_query.reshape(requests, NEW, heads_local, HD)
    first_place = seq_index * clen_dev

    def cached_part(request):
        query_block, key_block, value_block, length = request
        scores = (
            jnp.einsum("qhd,khd->hqk", query_block, key_block, preferred_element_type=jnp.float32)
            * scaling
        )
        visible = (first_place + lax.iota(jnp.int32, clen_dev) < length)[None, None, :]
        return block_partial(scores, visible, value_block)

    max_cached, sum_cached, out_cached = lax.map(
        cached_part,
        (
            grouped,
            cache_keys.reshape(requests, clen_dev, heads_local, HD),
            cache_values.reshape(requests, clen_dev, heads_local, HD),
            cache_lengths,
        ),
    )
    max_cached = jnp.transpose(max_cached, (0, 2, 1))
    sum_cached = jnp.transpose(sum_cached, (0, 2, 1))
    own_start = seq_index * tok_dev
    own_request = own_start // NEW
    offset = own_start % NEW
    own_queries = lax.dynamic_index_in_dim(grouped, own_request, 0, keepdims=False)
    new_scores = (
        jnp.einsum(
            "qhd,khd->hqk",
            own_queries,
            new_keys.reshape(tok_dev, heads_local, HD),
            preferred_element_type=jnp.float32,
        )
        * scaling
    )
    visible_new = (
        lax.iota(jnp.int32, NEW)[:, None] >= offset + lax.iota(jnp.int32, tok_dev)[None, :]
    )[None]
    max_new, sum_new, out_new = block_partial(
        new_scores, visible_new, new_values.reshape(tok_dev, heads_local, HD)
    )
    chosen_request = (lax.iota(jnp.int32, requests) == own_request)[:, None, None]
    max_placed = jnp.where(chosen_request, jnp.transpose(max_new)[None], negative)
    sum_placed = jnp.where(chosen_request, jnp.transpose(sum_new)[None], 0.0)
    out_placed = jnp.where(chosen_request[..., None], out_new[None], 0.0)
    local_max = jnp.maximum(max_cached, max_placed)
    factor_cached = jnp.exp(max_cached - local_max)
    factor_new = jnp.exp(max_placed - local_max)
    local_sum = sum_cached * factor_cached + sum_placed * factor_new
    local_out = out_cached * factor_cached[..., None] + out_placed * factor_new[..., None]
    flat_max = local_max.reshape(tokens, heads_local)
    row_max = lax.pmax(flat_max.astype(jnp.bfloat16), "seq").astype(flat_max.dtype)
    factors = jnp.exp(flat_max - row_max)
    weighted, row_sum = (
        lax.psum_scatter(
            (local_out.reshape(tokens, heads_local, HD) * factors[..., None]).astype(jnp.bfloat16),
            "seq",
            scatter_dimension=0,
            tiled=True,
        ).astype(jnp.float32),
        lax.psum_scatter(
            (local_sum.reshape(tokens, heads_local) * factors).astype(jnp.bfloat16),
            "seq",
            scatter_dimension=0,
            tiled=True,
        ).astype(jnp.float32),
    )
    attended = (
        (weighted / row_sum[..., None]).astype(jnp.bfloat16).reshape(tok_dev, heads_local * HD)
    )
    projected = jnp.dot(attended, out_proj, preferred_element_type=jnp.float32)
    attn_out = lax.psum_scatter(
        projected.astype(jnp.bfloat16), "tensor", scatter_dimension=1, tiled=True
    ).astype(jnp.float32)
    stream = residual.astype(jnp.float32) + attn_out
    square_total = lax.psum(jnp.sum(stream * stream, 1), "tensor")
    inverse_rms = lax.rsqrt(square_total / D + epsilon)
    normed = (stream * inverse_rms[:, None] * norm_gain).astype(jnp.bfloat16)
    logits = lax.psum(
        jnp.dot(normed, router, preferred_element_type=jnp.float32).astype(jnp.bfloat16), "tensor"
    ).astype(jnp.float32)
    matches = expert_ids[:, :, None] == lax.iota(jnp.int32, experts)[None, None, :]
    selected = jnp.sum(jnp.where(matches, logits[:, None, :], 0.0), 2)
    sigmoids = jax.nn.sigmoid(selected)
    gates = sigmoids / jnp.sum(sigmoids, 1, keepdims=True)
    normed_full = lax.all_gather(normed, "tensor", axis=1, tiled=True)
    shared_pair = jnp.einsum(
        "td,dcf->tcf", normed_full, shared_gate_up, preferred_element_type=jnp.float32
    )
    shared_act = (jax.nn.silu(shared_pair[:, 0]) * shared_pair[:, 1]).astype(jnp.bfloat16)
    shared_term = jnp.dot(shared_act, shared_down, preferred_element_type=jnp.float32)
    shared_out = lax.psum_scatter(
        shared_term.astype(jnp.bfloat16), "tensor", scatter_dimension=1, tiled=True
    ).astype(jnp.float32)
    cap = tensor_count * (
        (4 * tok_dev * topk + 3 * experts * tensor_count - 1) // (3 * experts * tensor_count)
    )
    flat_ids = expert_ids.reshape(-1)
    marks = (flat_ids[:, None] == lax.iota(jnp.int32, experts)[None, :]).astype(jnp.int32)
    earlier = jnp.cumsum(marks, 0) - marks
    rank = jnp.sum(earlier * marks, 1)
    slot_index = flat_ids * cap + rank
    source_rows = (
        jnp.full((experts * cap,), tok_dev, jnp.int32)
        .at[slot_index]
        .set(lax.iota(jnp.int32, flat_ids.shape[0]) // topk)
    )
    padded_local = jnp.concatenate([normed, jnp.zeros((1, width_local), jnp.bfloat16)], 0)
    outgoing = padded_local[source_rows].reshape(seq_count, exp_dev, cap, width_local)
    incoming = lax.all_to_all(outgoing, "seq", split_axis=0, concat_axis=0, tiled=True)
    routed_rows = lax.all_gather(incoming, "tensor", axis=3, tiled=True)
    expert_pair = jnp.einsum(
        "secd,edjf->secjf", routed_rows, expert_gate_up, preferred_element_type=jnp.float32
    )
    expert_act = (jax.nn.silu(expert_pair[..., 0, :]) * expert_pair[..., 1, :]).astype(jnp.bfloat16)
    expert_term = jnp.einsum(
        "secf,efd->secd", expert_act, expert_down, preferred_element_type=jnp.float32
    )
    expert_total = lax.psum_scatter(
        expert_term.astype(jnp.bfloat16), "tensor", scatter_dimension=3, tiled=True
    )
    returned = lax.all_to_all(expert_total, "seq", split_axis=0, concat_axis=0, tiled=True)
    picked = returned.reshape(experts * cap, width_local)[slot_index].reshape(
        tok_dev, topk, width_local
    )
    mixture = jnp.sum(gates[..., None] * picked.astype(jnp.float32), 1)
    return (stream + shared_out + mixture).astype(jnp.bfloat16)


def solution(mesh):
    in_specs = (
        P("seq", "tensor"),
        P("seq", "tensor"),
        P("seq", "tensor"),
        P("seq", "tensor"),
        P(None, "seq", "tensor"),
        P(None, "seq", "tensor"),
        P(),
        P("tensor", None),
        P("tensor"),
        P("tensor", None),
        P("seq", None),
        P("seq", None, None, "tensor"),
        P("seq", "tensor", None),
        P(None, None, "tensor"),
        P("tensor", None),
    )
    out_specs = P("seq", "tensor")
    return jax.shard_map(shards, mesh=mesh, in_specs=in_specs, out_specs=out_specs, check_vma=False)
```

profile of v0, /device:TPU:12, one launch (start us, length us, event | category | flops | bytes accessed | tf_op | source)
XLA Modules:
  0.0 633.3 jit_solution(6344024644250426973)
XLA Ops:
  7.3 6.3 copy.76
  13.6 6.2 copy.77
  20.5 66.9 %all-gather.3.cloned.1.call-done = bf16[2048,1024]{1,0:T(8,128)(2,1)} async-done(((bf16[128,1024]{1,0:T(8,128)(2,1)}), bf16[2048,1024]{1,0:T(8,128)(2,1)}) %all-gather.3.cloned.1.call-update) | async-done | bytes 4194320 | tf_op jit(solution)/shard_map/all_gather | solution.py:59
  87.4 5.3 copy.119
  92.6 77.7 %while.15 = (s32[]{:T(128)}, f32[4,8,512]{2,1,0:T(8,128)S(1)}, f32[4,8,512]{2,1,0:T(8,128)}, f32[4,512,8,128]{3,2,1,0:T(8,128)}, s32[]{:T(128)}, /*index=5*/s32[...) while((s32[]{:T(128)}, f32[4,8,512]{2,1,0:T(8,128)S(1)}, ...), condition=%wide.region_3.4_spmd.clone, body=%wide.region_0.3_spmd.sunk.clone | while | flops 1100997632 | bytes 41027724 | solution.py:72
  95.2 3.3 select_reduce_fusion.5
  101.4 4.7 fusion.94
  114.6 3.3 select_reduce_fusion.5
  120.8 4.7 fusion.94
  134.0 3.3 select_reduce_fusion.5
  140.2 4.7 fusion.94
  159.6 4.7 fusion.94
  183.0 64.5 %pmax.7 = bf16[2048,8]{0,1:T(8,128)(2,1)S(1)} all-reduce(bf16[2048,8]{0,1:T(8,128)(2,1)S(1)} %convert_element_type.81), channel_id=1, replica_groups=mesh['seq'=16,'tensor'=2] {'seq'}, use_global_device_ids=true, to_apply=%region_5.6 | all-reduce | flops 16384 | bytes 65536 | tf_op jit(solution)/shard_map/pmax | solution.py:112
  250.0 7.0 %multiply_add_fusion = f32[4,512,8,128]{3,2,1,0:T(8,128)S(1)} fusion(f32[4,512,8,128]{3,2,1,0:T(8,128)} %get-tuple-element.54, f32[4,512,8]{2,1,0:T(8,128)} %copy.88, f32[512,8,128]{2,1,0:T(8,128)} %copy.87, f32[4,512,8]{2,1,0:T(8,128)} %copy.83, pred[4]{0:T(512)(128)(4,1)S(1)} %copy-done.12), kind=kLoop, calls=%fused_computation.29 | loop fusion | flops 8388608 | bytes 19005444 | tf_op jit(solution)/shard_map/add | solution.py:110
  257.0 4.4 fusion.19
  262.5 60.0 %reduce-scatter.16.cloned.1.call-done = bf16[128,8]{1,0:T(8,128)(2,1)} async-done(((bf16[2048,8]{1,0:T(8,128)(2,1)}), bf16[128,8]{1,0:T(8,128)(2,1)}) %reduce-scatter.16.cloned.1.call-update) | async-done | bytes 2064
  323.4 100.9 %reduce-scatter.8.cloned.1.call-done = bf16[128,8,128]{2,1,0:T(8,128)(2,1)} async-done(((bf16[2048,8,128]{2,1,0:T(8,128)(2,1)}), bf16[128,8,128]{2,1,0:T(8,128)(2,1)}) %reduce-scatter.8.cloned.1.call-update) | async-done | bytes 262160 | tf_op jit(solution)/shard_map/reduce_scatter | solution.py:115
  425.5 3.7 convolution_convert_fusion.1
  431.8 3.4 scatter_custom_fusion
  435.2 4.0 reduce-scatter.10.cloned.1.call-done
  443.8 5.4 gather_fusion
  449.2 55.1 %all_to_all.10 = bf16[16,2,32,1024]{3,2,1,0:T(8,128)(2,1)S(1)} all-to-all(bf16[16,2,32,1024]{3,2,1,0:T(8,128)(2,1)} %bitcast.180), channel_id=1, replica_groups=mesh['seq'=16,'tensor'=2] {'seq'}, dimensions={0} | all-to-all | bytes 4194304 | tf_op jit(solution)/shard_map/all_to_all | solution.py:170
  505.9 13.1 %all-gather.5.cloned.1.call-done = bf16[16,2,32,2048]{3,2,0,1:T(8,128)(2,1)} async-done(((bf16[16,2,32,1024]{3,2,0,1:T(8,128)(2,1)}), bf16[16,2,32,2048]{3,2,0,1:T(8,128)(2,1)}) %all-gather.5.cloned.1.call-update) | async-done | bytes 4194320 | tf_op jit(solution)/shard_map/all_gather | solution.py:171
  518.9 10.8 %fusion.27 = f32[16,2,32,2,704]{4,2,3,0,1:T(8,128)S(1)} fusion(bf16[2,2048,2,704]{1,3,2,0:T(8,128)(2,1)} %param.28, bf16[16,2,32,2048]{3,2,0,1:T(8,128)(2,1)} %all-gather.5.cloned.1.call-done), kind=kOutput, calls=%fused_computation.39 | convolution fusion | flops 5905580032 | bytes 21495808 | tf_op jit(solution)/shard_map/secd,edjf->secjf/dot_general | solution.py:172
  529.8 7.9 %convert_bitcast_fusion = bf16[16,2,32,2048]{3,2,0,1:T(8,128)(2,1)} fusion(bf16[2,704,2048]{2,1,0:T(8,128)(2,1)} %param.29, f32[16,2,32,2,704]{4,2,3,0,1:T(8,128)S(1)} %fusion.27), kind=kOutput, calls=%fused_computation.34 | convolution fusion | flops 2959212544 | bytes 15728640 | tf_op jit(solution)/shard_map/secf,efd->secd/dot_general | solution.py:176
  537.7 13.5 %reduce-scatter.14.cloned.1.call-done = bf16[16,2,32,1024]{3,2,0,1:T(8,128)(2,1)} async-done(((bf16[16,2,32,2048]{3,2,0,1:T(8,128)(2,1)}), bf16[16,2,32,1024]{3,2,0,1:T(8,128)(2,1)}) %reduce-scatter.14.cloned.1.call-update) | async-done | bytes 2097168 | tf_op jit(solution)/shard_map/reduce_scatter | solution.py:179
  554.3 7.0 %all-to-all-start.1 = ((bf16[16,2,32,1024]{3,2,1,0:T(8,128)(2,1)}), bf16[16,2,32,1024]{3,2,1,0:T(8,128)(2,1)}, u32[]{:S(2)}, u32[]{:S(2)}) async-start(bf16[16,2,32,1024]{3,2,1,0:T(8,128)(2,1)} %copy.98), calls=%async_computation.5 | async-start | bytes 4194304 | tf_op jit(solution)/shard_map/all_to_all | solution.py:182
  563.7 4.3 fusion.44
  572.5 37.3 %all-to-all-done.1 = bf16[16,2,32,1024]{3,2,1,0:T(8,128)(2,1)} async-done(((bf16[16,2,32,1024]{3,2,1,0:T(8,128)(2,1)}), bf16[16,2,32,1024]{3,2,1,0:T(8,128)(2,1)}, u32[]{:S(2)}, u32[]{:S(2)}) %all-to-all-start.1) | async-done | bytes 2097184 | tf_op jit(solution)/shard_map/all_to_all | solution.py:182
  609.8 6.4 %gather_fusion.1 = bf16[768,1024]{1,0:T(8,128)(2,1)} fusion(bf16[1024,1024]{1,0:T(8,128)(2,1)} %bitcast.34, s32[1024]{0:T(1024)S(1)} %pad_clamp_fusion), kind=kCustom, calls=%fused_computation.1 | custom fusion | bytes 3148800 | tf_op jit(solution)/shard_map/gather | solution.py:183
  616.2 3.9 reshape.167
  620.2 4.4 multiply_reduce_fusion
  (125 shorter events, 89.2 us)
Async XLA Ops:
  6.5 561.6 %copy-start = (bf16[704,2048]{1,0:T(8,128)(2,1)S(1)}, bf16[704,2048]{1,0:T(8,128)(2,1)}, u32[]{:S(2)}) copy-start(bf16[704,2048]{1,0:T(8,128)(2,1)} %param.31) | copy-start | bytes 8650756
  6.5 80.8 %all-gather.3.cloned.1.call-start = ((), (), s32[]{:S(2)}) async-start(), calls=%async_computation.7 | async-start | bytes 4456448 | tf_op jit(solution)/shard_map/all_gather | solution.py:59
  7.3 315.2 %reduce-scatter.16.cloned.1.call-start = ((), (), s32[]{:S(2)}) async-start(), calls=%async_computation.13 | async-start | bytes 557056
  87.4 5.3 copy-start.13
  170.3 4.9 copy-start.8
  170.3 4.9 copy-start.11
  171.7 5.0 copy-start.6
  173.3 1.4 copy-start.1
  179.0 70.9 %copy-start.12 = (pred[4]{0:T(512)(128)(4,1)S(1)}, pred[4]{0:T(512)(128)(4,1)}, u32[]{:S(2)}) copy-start(pred[4]{0:T(512)(128)(4,1)} %iota_compare_fusion.4) | copy-start | bytes 16
  249.9 174.4 %reduce-scatter.8.cloned.1.call-start = ((), (), s32[]{:S(2)}) async-start(), calls=%async_computation.8 | async-start | bytes 4456448 | tf_op jit(solution)/shard_map/reduce_scatter | solution.py:115
  250.0 7.0 %copy-start.2 = (f32[2048,8]{1,0:T(8,128)S(1)}, f32[2048,8]{1,0:T(8,128)}, u32[]{:S(2)}) copy-start(f32[2048,8]{1,0:T(8,128)} %copy.89) | copy-start | bytes 196612
  261.4 0.7 copy-start.9
  261.5 177.7 %copy-start.3 = (bf16[128,1024]{1,0:T(8,128)(2,1)S(1)}, bf16[128,1024]{1,0:T(8,128)(2,1)}, u32[]{:S(2)}) copy-start(bf16[128,1024]{1,0:T(8,128)(2,1)} %param.17) | copy-start | bytes 786436
  261.5 181.3 %copy-start.10 = (f32[1024]{0:T(1024)S(1)}, f32[1024]{0:T(1024)}, u32[]{:S(2)}) copy-start(f32[1024]{0:T(1024)} %param.25) | copy-start | bytes 12292
  261.5 177.7 %reduce-scatter.10.cloned.1.call-start = ((), (), s32[]{:S(2)}) async-start(), calls=%async_computation.9 | async-start | bytes 786432 | tf_op jit(solution)/shard_map/reduce_scatter | solution.py:132
  429.2 89.7 %all-gather.5.cloned.1.call-start = ((), (), s32[]{:S(2)}) async-start(), calls=%async_computation.11 | async-start | bytes 6291456 | tf_op jit(solution)/shard_map/all_gather | solution.py:171
  505.8 45.4 %reduce-scatter.14.cloned.1.call-start = ((), (), s32[]{:S(2)}) async-start(), calls=%async_computation.12 | async-start | bytes 6291456 | tf_op jit(solution)/shard_map/reduce_scatter | solution.py:179
  554.3 55.5 %all-to-all-start.1 = ((bf16[16,2,32,1024]{3,2,1,0:T(8,128)(2,1)}), bf16[16,2,32,1024]{3,2,1,0:T(8,128)(2,1)}, u32[]{:S(2)}, u32[]{:S(2)}) async-start(bf16[16,2,32,1024]{3,2,1,0:T(8,128)(2,1)} %copy.98), calls=%async_computation.5 | async-start | bytes 4194304 | tf_op jit(solution)/shard_map/all_to_all | solution.py:182
  561.3 63.2 %reduce-scatter.12.cloned.1.call-start = ((), (), s32[]{:S(2)}) async-start(), calls=%async_computation.10 | async-start | bytes 786432 | tf_op jit(solution)/shard_map/reduce_scatter | solution.py:152
  563.7 5.9 copy-start.7
  616.2 8.3 %copy-start.4 = (bf16[128,1024]{1,0:T(8,128)(2,1)S(1)}, bf16[128,1024]{1,0:T(8,128)(2,1)}, u32[]{:S(2)}) copy-start(bf16[128,1024]{1,0:T(8,128)(2,1)} %param.17) | copy-start | bytes 786436
  616.2 8.3 %copy-start.5 = (bf16[128,1024]{1,0:T(8,128)(2,1)S(1)}, bf16[128,1024]{1,0:T(8,128)(2,1)}, u32[]{:S(2)}) copy-start(bf16[128,1024]{1,0:T(8,128)(2,1)} %reduce-scatter.10.cloned.1.call-done) | copy-start | bytes 786436
Sparse Core Ops, SparseCore 0:
  10.1 77.1 all-gather.2
  250.1 72.3 reduce-scatter.15
  324.9 99.4 reduce-scatter.7
  429.4 9.7 reduce-scatter.9
  505.9 12.9 all-gather.4
  537.8 13.3 reduce-scatter.13
  569.7 9.0 reduce-scatter.11
where the time goes:
time: 635 us; the launch traced here: 633 us
  waiting for transfers between devices  296 us (47%)
  blocking collectives  127 us (20%)
  local copies, waits for them, and re-layouts  88.5 us (14%)
  matrix products  64.3 us (10%)
  other arithmetic  36 us (6%)
  between operations  13.8 us (2%)
  starting transfers between devices  7.2 us (1%)
    reduce_scatter x1, waiting for transfers between devices, shards(): lax.psum_scatter((local_out.reshape(tokens, heads_local, HD) * factors[.....  101 us
    all_gather x1, waiting for transfers between devices, shards(): every_query = lax.all_gather(queries, 'seq', axis=0, tiled=True)  66.9 us
    pmax x1, blocking collectives, shards(): lax.pmax(flat_max.astype(jnp.bfloat16), 'seq').astype(flat_max.dtype)  64.5 us
    unnamed x8, waiting for transfers between devices  60.8 us
    all_to_all x1, blocking collectives, shards(): lax.all_to_all(outgoing, 'seq', split_axis=0, concat_axis=0, tiled=True)  55.1 us
    all_to_all x1, waiting for transfers between devices, shards(): lax.all_to_all(expert_total, 'seq', split_axis=0, concat_axis=0, tiled=True)  37.3 us
    dynamic_update_slice x12, local copies, waits for them, and re-layouts, shards(): lax.map(cached_part, (grouped, cache_keys.reshape(requests, clen_dev, hea...  26.4 us
    unnamed x34, local copies, waits for them, and re-layouts  21.7 us
  transfers between devices with their start and end apart: 8, of which 7 were waited for; matrix products, arithmetic and copies ran while one was open for 8% of the time, Pallas kernels for 0%

commit v1 on v0

v1 whole, which is shorter than its diff:
```python
import math

import jax
import jax.numpy as jnp
from jax import lax
from jax.experimental import pallas as pl
from jax.experimental.pallas import tpu as pltpu
from jax.sharding import PartitionSpec as P

D = 2048
HD = 128
NEW = 512


negative = -1e30
epsilon = 1e-06


LOG2E = 1.4426950408889634
STAT_ROWS = 16


def attention_kernel(
    tok_dev, len_ref, q_ref, k_ref, v_ref, nk_ref, nv_ref, out_ref
):
    request = pl.program_id(0)
    seq_index = lax.axis_index("seq")
    own_start = seq_index * tok_dev
    clen_dev = k_ref.shape[1]
    rows = q_ref.shape[0]
    quarters = rows // tok_dev
    own = own_start // rows == request
    remaining = len_ref[request] - seq_index * clen_dev
    scale = LOG2E / math.sqrt(HD)

    def scored(keys):
        return (
            lax.dot_general(
                keys, q_ref[...], (((1,), (1,)), ((), ())), preferred_element_type=jnp.float32
            )
            * scale
        )

    def weighted(weights, values):
        return lax.dot_general(
            weights.astype(jnp.bfloat16),
            values,
            (((0,), (0,)), ((), ())),
            preferred_element_type=jnp.float32,
        )

    def emit(out, top, total):
        high = total.astype(jnp.bfloat16).astype(jnp.float32)
        row = lax.broadcasted_iota(jnp.int32, (STAT_ROWS, rows), 0)
        stats = jnp.where(
            row == 0, top, jnp.where(row == 1, high, jnp.where(row == 2, total - high, 0.0))
        ).astype(jnp.bfloat16)
        for part in range(quarters):
            window = slice(part * tok_dev, (part + 1) * tok_dev)
            out_ref[part, :tok_dev, :] = out[window].astype(jnp.bfloat16)
            out_ref[part, tok_dev:, :] = stats[:, window]

    def rounded(top):
        return top.astype(jnp.bfloat16).astype(jnp.float32)

    visible = lax.broadcasted_iota(jnp.int32, (clen_dev, rows), 0) < remaining

    @pl.when(own)
    def _():
        cached = jnp.where(visible, scored(k_ref[0]), negative)
        place = lax.broadcasted_iota(jnp.int32, (tok_dev, rows), 0) + own_start % rows
        seen = place <= lax.broadcasted_iota(jnp.int32, (tok_dev, rows), 1)
        fresh = jnp.where(seen, scored(nk_ref[...]), negative)
        top = rounded(
            jnp.maximum(jnp.max(cached, 0, keepdims=True), jnp.max(fresh, 0, keepdims=True))
        )
        cached = jnp.where(visible, jnp.exp2(cached - top), 0.0)
        fresh = jnp.where(seen, jnp.exp2(fresh - top), 0.0)
        total = jnp.sum(cached, 0, keepdims=True) + jnp.sum(fresh, 0, keepdims=True)
        emit(weighted(cached, v_ref[0]) + weighted(fresh, nv_ref[...]), top, total)

    @pl.when(jnp.logical_not(own) & (remaining > 0))
    def _():
        cached = jnp.where(visible, scored(k_ref[0]), negative)
        top = rounded(jnp.max(cached, 0, keepdims=True))
        cached = jnp.where(visible, jnp.exp2(cached - top), 0.0)
        emit(weighted(cached, v_ref[0]), top, jnp.sum(cached, 0, keepdims=True))

    @pl.when(jnp.logical_not(own) & (remaining <= 0))
    def _():
        emit(
            jnp.zeros((rows, HD), jnp.float32),
            jnp.full((1, rows), negative, jnp.float32),
            jnp.zeros((1, rows), jnp.float32),
        )


def attention(lengths, every_query, cache_keys, cache_values, new_keys, new_values):
    requests, clen_dev, width = cache_keys.shape
    tok_dev = new_keys.shape[0]
    tokens = every_query.shape[0]
    heads = width // HD
    quarters = NEW // tok_dev
    return pl.pallas_call(
        lambda *refs: attention_kernel(tok_dev, *refs),
        grid_spec=pltpu.PrefetchScalarGridSpec(
            num_scalar_prefetch=1,
            grid=(requests, heads),
            in_specs=[
                pl.BlockSpec((NEW, HD), lambda r, h, n: (r, h)),
                pl.BlockSpec((1, clen_dev, HD), lambda r, h, n: (r, 0, h)),
                pl.BlockSpec((1, clen_dev, HD), lambda r, h, n: (r, 0, h)),
                pl.BlockSpec((tok_dev, HD), lambda r, h, n: (0, h)),
                pl.BlockSpec((tok_dev, HD), lambda r, h, n: (0, h)),
            ],
            out_specs=pl.BlockSpec(
                (quarters, tok_dev + STAT_ROWS, HD), lambda r, h, n: (r, 0, h)
            ),
        ),
        out_shape=jax.ShapeDtypeStruct(
            (tokens // tok_dev, tok_dev + STAT_ROWS, width), jnp.bfloat16
        ),
        compiler_params=pltpu.CompilerParams(vmem_limit_bytes=32 * 1024 * 1024),
        cost_estimate=pl.CostEstimate(
            flops=4 * NEW * clen_dev * width * 2,
            bytes_accessed=16 * 1024 * 1024,
            transcendentals=2 * NEW * clen_dev * heads,
        ),
        name="ragged_attention",
    )(lengths, every_query, cache_keys, cache_values, new_keys, new_values)


def combine_kernel(parts_ref, out_ref):
    sources = parts_ref.shape[0]
    tok_dev = out_ref.shape[0]
    stats = [
        parts_ref[source, tok_dev:, :].astype(jnp.float32) for source in range(sources)
    ]
    tops = jnp.concatenate([stat[0:1] for stat in stats], 0)
    sums = jnp.concatenate([stat[1:2] + stat[2:3] for stat in stats], 0)
    factors = jnp.exp2(tops - jnp.max(tops, 0, keepdims=True))
    factors = factors / jnp.sum(factors * sums, 0, keepdims=True)
    columns = factors.T
    total = jnp.zeros((tok_dev, HD), jnp.float32)
    for source in range(sources):
        total += columns[:, source : source + 1] * parts_ref[source, :tok_dev, :].astype(
            jnp.float32
        )
    out_ref[...] = total.astype(jnp.bfloat16)


def combine(parts):
    sources, rows, width = parts.shape
    tok_dev = rows - STAT_ROWS
    return pl.pallas_call(
        combine_kernel,
        grid=(width // HD,),
        in_specs=[pl.BlockSpec((sources, rows, HD), lambda h: (0, 0, h))],
        out_specs=pl.BlockSpec((tok_dev, HD), lambda h: (0, h)),
        out_shape=jax.ShapeDtypeStruct((tok_dev, width), jnp.bfloat16),
        compiler_params=pltpu.CompilerParams(vmem_limit_bytes=32 * 1024 * 1024),
        name="combine_blocks",
    )(parts)


def shards(
    residual,
    queries,
    new_keys,
    new_values,
    cache_keys,
    cache_values,
    cache_lengths,
    out_proj,
    norm_gain,
    router,
    expert_ids,
    expert_gate_up,
    expert_down,
    shared_gate_up,
    shared_down,
):
    seq_count = lax.axis_size("seq")
    tensor_count = lax.axis_size("tensor")
    tok_dev = queries.shape[0]
    width_local = residual.shape[1]
    experts = router.shape[1]
    exp_dev = expert_gate_up.shape[0]
    topk = expert_ids.shape[1]
    every_query = lax.all_gather(queries, "seq", axis=0, tiled=True)
    partials = attention(
        cache_lengths, every_query, cache_keys, cache_values, new_keys, new_values
    )
    attended = combine(
        lax.all_to_all(partials, "seq", split_axis=0, concat_axis=0, tiled=True)
    )
    projected = jnp.dot(attended, out_proj, preferred_element_type=jnp.float32)
    attn_out = lax.psum_scatter(
        projected.astype(jnp.bfloat16), "tensor", scatter_dimension=1, tiled=True
    ).astype(jnp.float32)
    stream = residual.astype(jnp.float32) + attn_out
    square_total = lax.psum(jnp.sum(stream * stream, 1), "tensor")
    inverse_rms = lax.rsqrt(square_total / D + epsilon)
    normed = (stream * inverse_rms[:, None] * norm_gain).astype(jnp.bfloat16)
    logits = lax.psum(
        jnp.dot(normed, router, preferred_element_type=jnp.float32).astype(jnp.bfloat16), "tensor"
    ).astype(jnp.float32)
    matches = expert_ids[:, :, None] == lax.iota(jnp.int32, experts)[None, None, :]
    selected = jnp.sum(jnp.where(matches, logits[:, None, :], 0.0), 2)
    sigmoids = jax.nn.sigmoid(selected)
    gates = sigmoids / jnp.sum(sigmoids, 1, keepdims=True)
    normed_full = lax.all_gather(normed, "tensor", axis=1, tiled=True)
    shared_pair = jnp.einsum(
        "td,dcf->tcf", normed_full, shared_gate_up, preferred_element_type=jnp.float32
    )
    shared_act = (jax.nn.silu(shared_pair[:, 0]) * shared_pair[:, 1]).astype(jnp.bfloat16)
    shared_term = jnp.dot(shared_act, shared_down, preferred_element_type=jnp.float32)
    shared_out = lax.psum_scatter(
        shared_term.astype(jnp.bfloat16), "tensor", scatter_dimension=1, tiled=True
    ).astype(jnp.float32)
    cap = tensor_count * (
        (4 * tok_dev * topk + 3 * experts * tensor_count - 1) // (3 * experts * tensor_count)
    )
    flat_ids = expert_ids.reshape(-1)
    marks = (flat_ids[:, None] == lax.iota(jnp.int32, experts)[None, :]).astype(jnp.int32)
    earlier = jnp.cumsum(marks, 0) - marks
    rank = jnp.sum(earlier * marks, 1)
    slot_index = flat_ids * cap + rank
    source_rows = (
        jnp.full((experts * cap,), tok_dev, jnp.int32)
        .at[slot_index]
        .set(lax.iota(jnp.int32, flat_ids.shape[0]) // topk)
    )
    padded_local = jnp.concatenate([normed, jnp.zeros((1, width_local), jnp.bfloat16)], 0)
    outgoing = padded_local[source_rows].reshape(seq_count, exp_dev, cap, width_local)
    incoming = lax.all_to_all(outgoing, "seq", split_axis=0, concat_axis=0, tiled=True)
    routed_rows = lax.all_gather(incoming, "tensor", axis=3, tiled=True)
    expert_pair = jnp.einsum(
        "secd,edjf->secjf", routed_rows, expert_gate_up, preferred_element_type=jnp.float32
    )
    expert_act = (jax.nn.silu(expert_pair[..., 0, :]) * expert_pair[..., 1, :]).astype(jnp.bfloat16)
    expert_term = jnp.einsum(
        "secf,efd->secd", expert_act, expert_down, preferred_element_type=jnp.float32
    )
    expert_total = lax.psum_scatter(
        expert_term.astype(jnp.bfloat16), "tensor", scatter_dimension=3, tiled=True
    )
    returned = lax.all_to_all(expert_total, "seq", split_axis=0, concat_axis=0, tiled=True)
    picked = returned.reshape(experts * cap, width_local)[slot_index].reshape(
        tok_dev, topk, width_local
    )
    mixture = jnp.sum(gates[..., None] * picked.astype(jnp.float32), 1)
    return (stream + shared_out + mixture).astype(jnp.bfloat16)


def solution(mesh):
    in_specs = (
        P("seq", "tensor"),
        P("seq", "tensor"),
        P("seq", "tensor"),
        P("seq", "tensor"),
        P(None, "seq", "tensor"),
        P(None, "seq", "tensor"),
        P(),
        P("tensor", None),
        P("tensor"),
        P("tensor", None),
        P("seq", None),
        P("seq", None, None, "tensor"),
        P("seq", "tensor", None),
        P(None, None, "tensor"),
        P("tensor", None),
    )
    out_specs = P("seq", "tensor")
    return jax.shard_map(shards, mesh=mesh, in_specs=in_specs, out_specs=out_specs, check_vma=False)
```

time: 635 us -> 455 us (0.72)
  blocking collectives: 127 us -> 62.4 us
  local copies, waits for them, and re-layouts: 88.5 us -> 36.1 us
  waiting for transfers between devices: 296 us -> 250 us
  matrix products: 64.3 us -> 26.2 us
  Pallas kernels: 0 us -> 30.3 us
  other arithmetic: 36 us -> 10.5 us
  starting transfers between devices: 7.2 us -> 25.5 us
    all_to_all x0 -> x1, waiting for transfers between devices: none -> 103 us  [shards(): lax.all_to_all(partials, 'seq', split_axis=0, concat_axis=0, tiled=True)]
    reduce_scatter x1 -> x0, waiting for transfers between devices: 101 us -> none  [shards(): lax.psum_scatter((local_out.reshape(tokens, heads_local, HD) * factors[.....]
    pmax x1 -> x0, blocking collectives: 64.5 us -> none  [shards(): lax.pmax(flat_max.astype(jnp.bfloat16), 'seq').astype(flat_max.dtype)]
    unnamed x8 -> x5, waiting for transfers between devices: 60.8 us -> 0.78 us
    dot_general x10 -> x0, matrix products: 35.9 us -> none  [the longest x5 21.1 us: block_partial(): jnp.einsum('hqk,khd->qhd', weights.astype(jnp.bfloat16), values, preferre...]
    pallas_call x0 -> x2, Pallas kernels: none -> 30.3 us  [the longest x1 23.1 us: attention(): pl.pallas_call(lambda *refs: attention_kernel(tok_dev, *refs), grid_spec=...]
    dynamic_update_slice x12 -> x0, local copies, waits for them, and re-layouts: 26.4 us -> none  [shards(): lax.map(cached_part, (grouped, cache_keys.reshape(requests, clen_dev, hea...]
    all_to_all x0 -> x1, starting transfers between devices: none -> 18.4 us  [shards(): lax.all_to_all(partials, 'seq', split_axis=0, concat_axis=0, tiled=True)]
  transfers between devices with their start and end apart: 8 -> 7, of which waited for: 7 -> 6; matrix products, arithmetic and copies ran while one was open for 8% -> 6% of each run, Pallas kernels for 0% -> 0%
where the time goes in v1:
time: 455 us; the launch traced here: 454 us
  waiting for transfers between devices  250 us (55%)
  blocking collectives  62.4 us (14%)
  local copies, waits for them, and re-layouts  36.1 us (8%)
  Pallas kernels  30.3 us (7%)
  matrix products  26.2 us (6%)
  starting transfers between devices  25.5 us (6%)
  between operations  13.3 us (3%)
  other arithmetic  10.5 us (2%)
    all_to_all x1, waiting for transfers between devices, shards(): lax.all_to_all(partials, 'seq', split_axis=0, concat_axis=0, tiled=True)  103 us
    all_gather x1, waiting for transfers between devices, shards(): every_query = lax.all_gather(queries, 'seq', axis=0, tiled=True)  80.1 us
    all_to_all x1, blocking collectives, shards(): lax.all_to_all(outgoing, 'seq', split_axis=0, concat_axis=0, tiled=True)  55.1 us
    all_to_all x1, waiting for transfers between devices, shards(): lax.all_to_all(expert_total, 'seq', split_axis=0, concat_axis=0, tiled=True)  37.3 us
    pallas_call x1, Pallas kernels, attention(): pl.pallas_call(lambda *refs: attention_kernel(tok_dev, *refs), grid_spec=...  23.1 us
    all_to_all x1, starting transfers between devices, shards(): lax.all_to_all(partials, 'seq', split_axis=0, concat_axis=0, tiled=True)  18.4 us
    reduce_scatter x1, waiting for transfers between devices, shards(): lax.psum_scatter(expert_term.astype(jnp.bfloat16), 'tensor', scatter_dime...  13.5 us
    all_gather x1, waiting for transfers between devices, shards(): routed_rows = lax.all_gather(incoming, 'tensor', axis=3, tiled=True)  13.1 us
  transfers between devices with their start and end apart: 7, of which 6 were waited for; matrix products, arithmetic and copies ran while one was open for 6% of the time, Pallas kernels for 0%

profile of v1, /device:TPU:12, one launch (start us, length us, event | category | flops | bytes accessed | tf_op | source)
XLA Modules:
  0.0 454.4 jit_solution(13196191030325047721)
XLA Ops:
  7.3 80.1 %all-gather.3.cloned.1.call-done.refs_1_ = bf16[2048,1024]{1,0:T(8,128)(2,1)} async-done(((bf16[128,1024]{1,0:T(8,128)(2,1)}), bf16[2048,1024]{1,0:T(8,128)(2,1)}) %all-gather.3.cloned.1.call-update) | async-done | bytes 4194320 | tf_op jit(solution)/shard_map/all_gather | solution.py:190
  87.4 2.2 copy-done.2
  89.5 2.2 copy-done.3
  91.7 2.2 copy-done.4
  96.5 23.1 %ragged_attention.1 = bf16[16,144,1024]{2,1,0:T(8,128)(2,1)S(1)} custom-call(s32[4]{0:T(128)S(1)} %copy-done.7, bf16[2048,1024]{1,0:T(8,128)(2,1)S(1)} %copy-done.4, bf16[4,512,1024]{2,1,0:T(8,128)(2,1)S(1)} %copy-done.2, bf16[4,512,1024]{2,1,0:T(8,128)(2,1)S(1)} %copy-done.3, bf16[128,1024]{1,0:T(8,128)(2,1)S(1)} %copy-done.5, bf16[128,1024]{1,0:T(8,128)(2,1)S(1)} %copy-done.6), custom_call_target="tpu_custom_call" | custom-call | flops 2147483648 | bytes 16777216 | tf_op jit(solution)/shard_map/ragged_attention/pallas_call | solution.py:104
  119.5 2.2 copy-done.1
  121.7 18.4 %all-to-all-start = ((bf16[16,144,1024]{2,1,0:T(8,128)(2,1)}), bf16[16,144,1024]{2,1,0:T(8,128)(2,1)}, u32[]{:S(2)}, u32[]{:S(2)}) async-start(bf16[16,144,1024]{2,1,0:T(8,128)(2,1)} %copy-done.1), calls=%async_computation | async-start | bytes 9437184 | tf_op jit(solution)/shard_map/all_to_all | solution.py:195
  140.5 103.3 %all-to-all-done.parts_ref = bf16[16,144,1024]{2,1,0:T(8,128)(2,1)} async-done(((bf16[16,144,1024]{2,1,0:T(8,128)(2,1)}), bf16[16,144,1024]{2,1,0:T(8,128)(2,1)}, u32[]{:S(2)}, u32[]{:S(2)}) %all-to-all-start) | async-done | bytes 4718624 | tf_op jit(solution)/shard_map/all_to_all | solution.py:195
  243.8 7.3 %combine_blocks.1 = bf16[128,1024]{1,0:T(8,128)(2,1)S(1)} custom-call(bf16[16,144,1024]{2,1,0:T(8,128)(2,1)} %all-to-all-done.parts_ref), custom_call_target="tpu_custom_call" | custom-call | tf_op jit(solution)/shard_map/combine_blocks/pallas_call | solution.py:155
  251.1 1.5 convolution_convert_fusion.1
  252.7 1.7 reduce-window.6
  255.2 3.4 scatter_custom_fusion
  258.6 1.9 reduce-scatter.4.cloned.1.call-done
  261.6 2.5 psum.14
  265.2 5.4 %gather_fusion = bf16[1024,1024]{1,0:T(8,128)(2,1)} fusion(bf16[129,1024]{1,0:T(8,128)(2,1)S(1)} %concatenate.3, s32[1024]{0:T(1024)S(1)} %fusion.28), kind=kCustom, calls=%fused_computation | custom fusion | bytes 4198400 | tf_op jit(solution)/shard_map/gather | solution.py:235
  270.5 55.1 %all_to_all.15 = bf16[16,2,32,1024]{3,2,1,0:T(8,128)(2,1)S(1)} all-to-all(bf16[16,2,32,1024]{3,2,1,0:T(8,128)(2,1)} %bitcast.82), channel_id=1, replica_groups=mesh['seq'=16,'tensor'=2] {'seq'}, dimensions={0} | all-to-all | bytes 4194304 | tf_op jit(solution)/shard_map/all_to_all | solution.py:236
  325.6 1.5 copy.42
  327.2 13.1 %all-gather.5.cloned.1.call-done = bf16[16,2,32,2048]{3,2,0,1:T(8,128)(2,1)} async-done(((bf16[16,2,32,1024]{3,2,0,1:T(8,128)(2,1)}), bf16[16,2,32,2048]{3,2,0,1:T(8,128)(2,1)}) %all-gather.5.cloned.1.call-update) | async-done | bytes 4194320 | tf_op jit(solution)/shard_map/all_gather | solution.py:237
  340.3 10.8 %fusion.9 = f32[16,2,32,2,704]{4,2,3,0,1:T(8,128)S(1)} fusion(bf16[2,2048,2,704]{1,3,2,0:T(8,128)(2,1)} %param.26, bf16[16,2,32,2048]{3,2,0,1:T(8,128)(2,1)} %all-gather.5.cloned.1.call-done), kind=kOutput, calls=%fused_computation.14 | convolution fusion | flops 5905580032 | bytes 21495808 | tf_op jit(solution)/shard_map/secd,edjf->secjf/dot_general | solution.py:238
  351.1 7.9 %convert_bitcast_fusion = bf16[16,2,32,2048]{3,2,0,1:T(8,128)(2,1)} fusion(bf16[2,704,2048]{2,1,0:T(8,128)(2,1)} %param.27, f32[16,2,32,2,704]{4,2,3,0,1:T(8,128)S(1)} %fusion.9), kind=kOutput, calls=%fused_computation.9 | convolution fusion | flops 2959212544 | bytes 15728640 | tf_op jit(solution)/shard_map/secf,efd->secd/dot_general | solution.py:242
  359.0 13.5 %reduce-scatter.8.cloned.1.call-done = bf16[16,2,32,1024]{3,2,0,1:T(8,128)(2,1)} async-done(((bf16[16,2,32,2048]{3,2,0,1:T(8,128)(2,1)}), bf16[16,2,32,1024]{3,2,0,1:T(8,128)(2,1)}) %reduce-scatter.8.cloned.1.call-update) | async-done | bytes 2097168 | tf_op jit(solution)/shard_map/reduce_scatter | solution.py:245
  372.5 3.2 copy.44
  375.7 7.0 %all-to-all-start.2 = ((bf16[16,2,32,1024]{3,2,1,0:T(8,128)(2,1)}), bf16[16,2,32,1024]{3,2,1,0:T(8,128)(2,1)}, u32[]{:S(2)}, u32[]{:S(2)}) async-start(bf16[16,2,32,1024]{3,2,1,0:T(8,128)(2,1)} %copy.44), calls=%async_computation.5 | async-start | bytes 4194304 | tf_op jit(solution)/shard_map/all_to_all | solution.py:248
  382.7 2.4 all_gather.10
  385.1 4.3 fusion.16
  389.4 1.5 convolution_convert_fusion
  391.1 2.5 psum.15
  393.8 37.3 %all-to-all-done.2 = bf16[16,2,32,1024]{3,2,1,0:T(8,128)(2,1)} async-done(((bf16[16,2,32,1024]{3,2,1,0:T(8,128)(2,1)}), bf16[16,2,32,1024]{3,2,1,0:T(8,128)(2,1)}, u32[]{:S(2)}, u32[]{:S(2)}) %all-to-all-start.2) | async-done | bytes 2097184 | tf_op jit(solution)/shard_map/all_to_all | solution.py:248
  431.2 6.4 %gather_fusion.1 = bf16[768,1024]{1,0:T(8,128)(2,1)} fusion(bf16[1024,1024]{1,0:T(8,128)(2,1)} %bitcast.15, s32[1024]{0:T(1024)S(1)} %pad_clamp_fusion), kind=kCustom, calls=%fused_computation.1 | custom fusion | bytes 3148800 | tf_op jit(solution)/shard_map/gather | solution.py:249
  437.6 3.9 reshape.84
  441.5 4.4 multiply_reduce_fusion
  445.9 2.0 add_convert_fusion
  (61 shorter events, 7.2 us)
Async XLA Ops:
  6.5 382.9 %copy-start = (bf16[704,2048]{1,0:T(8,128)(2,1)S(1)}, bf16[704,2048]{1,0:T(8,128)(2,1)}, u32[]{:S(2)}) copy-start(bf16[704,2048]{1,0:T(8,128)(2,1)} %param.29) | copy-start | bytes 8650756
  6.5 80.8 %all-gather.3.cloned.1.call-start = ((), (), s32[]{:S(2)}) async-start(), calls=%async_computation.6 | async-start | bytes 4456448 | tf_op jit(solution)/shard_map/all_gather | solution.py:190
  87.4 2.2 copy-start.2
  89.5 2.2 copy-start.3
  91.7 2.2 copy-start.4
  93.9 0.9 copy-start.5
  94.9 0.9 copy-start.6
  95.8 0.7 copy-start.7
  119.5 2.2 copy-start.1
  121.7 18.4 %copy-start.13 = (s32[128,6]{0,1:T(8,128)S(1)}, s32[128,6]{0,1:T(8,128)}, u32[]{:S(2)}) copy-start(s32[128,6]{0,1:T(8,128)} %param.25) | copy-start | bytes 9220
  121.7 122.1 %all-to-all-start = ((bf16[16,144,1024]{2,1,0:T(8,128)(2,1)}), bf16[16,144,1024]{2,1,0:T(8,128)(2,1)}, u32[]{:S(2)}, u32[]{:S(2)}) async-start(bf16[16,144,1024]{2,1,0:T(8,128)(2,1)} %copy-done.1), calls=%async_computation | async-start | bytes 9437184 | tf_op jit(solution)/shard_map/all_to_all | solution.py:195
  140.1 120.4 %reduce-scatter.4.cloned.1.call-start = ((), (), s32[]{:S(2)}) async-start(), calls=%async_computation.7 | async-start | bytes 786432 | tf_op jit(solution)/shard_map/reduce_scatter | solution.py:198
  243.8 7.3 %copy-start.8 = (bf16[1024,2048]{1,0:T(8,128)(2,1)S(1)}, bf16[1024,2048]{1,0:T(8,128)(2,1)}, u32[]{:S(2)}) copy-start(bf16[1024,2048]{1,0:T(8,128)(2,1)} %param.22) | copy-start | bytes 12582916
  251.1 9.4 %copy-start.9 = (bf16[128,1024]{1,0:T(8,128)(2,1)S(1)}, bf16[128,1024]{1,0:T(8,128)(2,1)}, u32[]{:S(2)}) copy-start(bf16[128,1024]{1,0:T(8,128)(2,1)} %param.15) | copy-start | bytes 786436
  251.1 12.9 %copy-start.14 = (f32[1024]{0:T(1024)S(1)}, f32[1024]{0:T(1024)}, u32[]{:S(2)}) copy-start(f32[1024]{0:T(1024)} %param.23) | copy-start | bytes 12292
  252.7 87.6 %all-gather.5.cloned.1.call-start = ((), (), s32[]{:S(2)}) async-start(), calls=%async_computation.9 | async-start | bytes 6291456 | tf_op jit(solution)/shard_map/all_gather | solution.py:237
  327.1 45.4 %reduce-scatter.8.cloned.1.call-start = ((), (), s32[]{:S(2)}) async-start(), calls=%async_computation.10 | async-start | bytes 6291456 | tf_op jit(solution)/shard_map/reduce_scatter | solution.py:245
  375.7 55.5 %all-to-all-start.2 = ((bf16[16,2,32,1024]{3,2,1,0:T(8,128)(2,1)}), bf16[16,2,32,1024]{3,2,1,0:T(8,128)(2,1)}, u32[]{:S(2)}, u32[]{:S(2)}) async-start(bf16[16,2,32,1024]{3,2,1,0:T(8,128)(2,1)} %copy.44), calls=%async_computation.5 | async-start | bytes 4194304 | tf_op jit(solution)/shard_map/all_to_all | solution.py:248
  382.7 63.2 %reduce-scatter.6.cloned.1.call-start = ((), (), s32[]{:S(2)}) async-start(), calls=%async_computation.8 | async-start | bytes 786432 | tf_op jit(solution)/shard_map/reduce_scatter | solution.py:218
  385.1 5.9 %copy-start.12 = (bf16[1024,32]{0,1:T(8,128)(2,1)S(1)}, bf16[1024,32]{0,1:T(8,128)(2,1)}, u32[]{:S(2)}) copy-start(bf16[1024,32]{0,1:T(8,128)(2,1)} %param.24) | copy-start | bytes 196612
  437.6 8.3 %copy-start.10 = (bf16[128,1024]{1,0:T(8,128)(2,1)S(1)}, bf16[128,1024]{1,0:T(8,128)(2,1)}, u32[]{:S(2)}) copy-start(bf16[128,1024]{1,0:T(8,128)(2,1)} %param.15) | copy-start | bytes 786436
  437.6 8.3 %copy-start.11 = (bf16[128,1024]{1,0:T(8,128)(2,1)S(1)}, bf16[128,1024]{1,0:T(8,128)(2,1)}, u32[]{:S(2)}) copy-start(bf16[128,1024]{1,0:T(8,128)(2,1)} %reduce-scatter.4.cloned.1.call-done) | copy-start | bytes 786436
Sparse Core Ops, SparseCore 0:
  10.1 77.1 all-gather.2
  252.8 7.6 reduce-scatter.3
  327.3 12.9 all-gather.4
  359.2 13.3 reduce-scatter.7
  391.0 9.0 reduce-scatter.5

commit v2 on v1

--- a/solution.py
+++ b/solution.py
@@ -95,11 +95,10 @@
         )
 
 
-def attention(lengths, every_query, cache_keys, cache_values, new_keys, new_values):
+def attention(first, heads, lengths, every_query, cache_keys, cache_values, new_keys, new_values):
     requests, clen_dev, width = cache_keys.shape
     tok_dev = new_keys.shape[0]
     tokens = every_query.shape[0]
-    heads = width // HD
     quarters = NEW // tok_dev
     return pl.pallas_call(
         lambda *refs: attention_kernel(tok_dev, *refs),
@@ -107,27 +106,132 @@
             num_scalar_prefetch=1,
             grid=(requests, heads),
             in_specs=[
-                pl.BlockSpec((NEW, HD), lambda r, h, n: (r, h)),
-                pl.BlockSpec((1, clen_dev, HD), lambda r, h, n: (r, 0, h)),
-                pl.BlockSpec((1, clen_dev, HD), lambda r, h, n: (r, 0, h)),
-                pl.BlockSpec((tok_dev, HD), lambda r, h, n: (0, h)),
-                pl.BlockSpec((tok_dev, HD), lambda r, h, n: (0, h)),
+                pl.BlockSpec((NEW, HD), lambda r, h, n: (r, first + h)),
+                pl.BlockSpec((1, clen_dev, HD), lambda r, h, n: (r, 0, first + h)),
+                pl.BlockSpec((1, clen_dev, HD), lambda r, h, n: (r, 0, first + h)),
+                pl.BlockSpec((tok_dev, HD), lambda r, h, n: (0, first + h)),
+                pl.BlockSpec((tok_dev, HD), lambda r, h, n: (0, first + h)),
             ],
             out_specs=pl.BlockSpec(
                 (quarters, tok_dev + STAT_ROWS, HD), lambda r, h, n: (r, 0, h)
             ),
         ),
         out_shape=jax.ShapeDtypeStruct(
-            (tokens // tok_dev, tok_dev + STAT_ROWS, width), jnp.bfloat16
+            (tokens // tok_dev, tok_dev + STAT_ROWS, heads * HD), jnp.bfloat16
         ),
         compiler_params=pltpu.CompilerParams(vmem_limit_bytes=32 * 1024 * 1024),
         cost_estimate=pl.CostEstimate(
-            flops=4 * NEW * clen_dev * width * 2,
+            flops=4 * requests * NEW * clen_dev * heads * HD * 4,
             bytes_accessed=16 * 1024 * 1024,
             transcendentals=2 * NEW * clen_dev * heads,
         ),
         name="ragged_attention",
     )(lengths, every_query, cache_keys, cache_values, new_keys, new_values)
+
+
+def gather_kernel(
+    own_ref, out_ref, local_sem, zs, zr, xs, xr, ys, yr, fs, fr, gs, gr
+):
+    rows = own_ref.shape[0]
+    half = rows // 2
+    planes = lax.axis_size("seq") // 4
+    me = lax.axis_index("seq")
+    plane, corner = me // 4, me % 4
+    side_x = corner + 1 - 2 * (corner % 2)
+    side_y = (corner + 2) % 4
+    step_by = jnp.where(plane < planes // 2, 1, planes - 1)
+
+    def plane_at(k):
+        return (plane + k * step_by) % planes
+
+    def rows_of(index, start=0, size=rows):
+        return pl.ds(pl.multiple_of(index * rows + start, half), size)
+
+    def copy(src, dst, send, recv, target):
+        return pltpu.make_async_remote_copy(
+            src_ref=src,
+            dst_ref=dst,
+            send_sem=send,
+            recv_sem=recv,
+            device_id={"seq": target},
+            device_id_type=pl.DeviceIdType.MESH,
+        )
+
+    barrier = pltpu.get_barrier_semaphore()
+    peers = [plane_at(k) * 4 + corner for k in range(1, planes)]
+    peers += [plane * 4 + side_x, plane * 4 + side_y]
+    for peer in peers:
+        pl.semaphore_signal(
+            barrier, inc=1, device_id={"seq": peer}, device_id_type=pl.DeviceIdType.MESH
+        )
+    pl.semaphore_wait(barrier, len(peers))
+
+    mine = pltpu.make_async_copy(own_ref, out_ref.at[rows_of(me)], local_sem)
+    mine.start()
+    sends = []
+    for k in range(1, planes):
+        target = plane_at(k)
+        send = copy(
+            own_ref, out_ref.at[rows_of(me)], zs.at[k], zr.at[plane], target * 4 + corner
+        )
+        send.start()
+        sends.append(send)
+
+    def arrived(index, start, size, sem):
+        place = out_ref.at[rows_of(index, start, size)]
+        pltpu.make_async_copy(place, place, sem).wait()
+
+    def forward(k):
+        level = plane_at(k)
+        from_y = level * 4 + side_y
+        arrived(from_y, 0, rows, yr.at[k])
+        place = out_ref.at[rows_of(from_y, 0, half)]
+        send = copy(place, place, fs.at[k], fr.at[k], plane * 4 + side_x)
+        send.start()
+        sends.append(send)
+        from_x = level * 4 + side_x
+        arrived(from_x, 0, rows, xr.at[k])
+        place = out_ref.at[rows_of(from_x, half, half)]
+        send = copy(place, place, gs.at[k], gr.at[k], plane * 4 + side_y)
+        send.start()
+        sends.append(send)
+
+    for k in range(planes):
+        level = plane_at(k)
+        index = level * 4 + corner
+        if k > 0:
+            arrived(index, 0, rows, zr.at[level])
+        place = out_ref.at[rows_of(index)]
+        source = own_ref if k == 0 else place
+        for send in (
+            copy(source, place, xs.at[k], xr.at[k], plane * 4 + side_x),
+            copy(source, place, ys.at[k], yr.at[k], plane * 4 + side_y),
+        ):
+            send.start()
+            sends.append(send)
+        if k > 0:
+            forward(k - 1)
+    forward(planes - 1)
+    diagonal = 3 - corner
+    for k in range(planes):
+        arrived(plane_at(k) * 4 + diagonal, 0, half, fr.at[k])
+        arrived(plane_at(k) * 4 + diagonal, half, half, gr.at[k])
+    for send in sends:
+        send.wait_send()
+    mine.wait()
+
+
+def gather_rows(rows, count):
+    planes = count // 4
+    return pl.pallas_call(
+        gather_kernel,
+        in_specs=[pl.BlockSpec(memory_space=pl.ANY)],
+        out_specs=pl.BlockSpec(memory_space=pl.ANY),
+        out_shape=jax.ShapeDtypeStruct((rows.shape[0] * count, rows.shape[1]), rows.dtype),
+        scratch_shapes=[pltpu.SemaphoreType.DMA] + [pltpu.SemaphoreType.DMA((planes,))] * 10,
+        compiler_params=pltpu.CompilerParams(collective_id=0, has_side_effects=True),
+        name="gather_rows",
+    )(rows)
 
 
 def combine_kernel(parts_ref, out_ref):
@@ -187,14 +291,29 @@
     experts = router.shape[1]
     exp_dev = expert_gate_up.shape[0]
     topk = expert_ids.shape[1]
-    every_query = lax.all_gather(queries, "seq", axis=0, tiled=True)
-    partials = attention(
-        cache_lengths, every_query, cache_keys, cache_values, new_keys, new_values
-    )
-    attended = combine(
-        lax.all_to_all(partials, "seq", split_axis=0, concat_axis=0, tiled=True)
-    )
-    projected = jnp.dot(attended, out_proj, preferred_element_type=jnp.float32)
+    every_query = gather_rows(queries, seq_count)
+    heads_local = queries.shape[1] // HD
+    pieces = 2 if heads_local % 2 == 0 else 1
+    heads_piece = heads_local // pieces
+    projected = 0.0
+    for piece in range(pieces):
+        partials = attention(
+            piece * heads_piece,
+            heads_piece,
+            cache_lengths,
+            every_query,
+            cache_keys,
+            cache_values,
+            new_keys,
+            new_values,
+        )
+        attended = combine(
+            lax.all_to_all(partials, "seq", split_axis=0, concat_axis=0, tiled=True)
+        )
+        features = slice(piece * heads_piece * HD, (piece + 1) * heads_piece * HD)
+        projected += jnp.dot(
+            attended, out_proj[features], preferred_element_type=jnp.float32
+        )
     attn_out = lax.psum_scatter(
         projected.astype(jnp.bfloat16), "tensor", scatter_dimension=1, tiled=True
     ).astype(jnp.float32)
@@ -226,30 +345,53 @@
     earlier = jnp.cumsum(marks, 0) - marks
     rank = jnp.sum(earlier * marks, 1)
     slot_index = flat_ids * cap + rank
-    source_rows = (
-        jnp.full((experts * cap,), tok_dev, jnp.int32)
-        .at[slot_index]
-        .set(lax.iota(jnp.int32, flat_ids.shape[0]) // topk)
-    )
-    padded_local = jnp.concatenate([normed, jnp.zeros((1, width_local), jnp.bfloat16)], 0)
-    outgoing = padded_local[source_rows].reshape(seq_count, exp_dev, cap, width_local)
-    incoming = lax.all_to_all(outgoing, "seq", split_axis=0, concat_axis=0, tiled=True)
-    routed_rows = lax.all_gather(incoming, "tensor", axis=3, tiled=True)
-    expert_pair = jnp.einsum(
-        "secd,edjf->secjf", routed_rows, expert_gate_up, preferred_element_type=jnp.float32
-    )
-    expert_act = (jax.nn.silu(expert_pair[..., 0, :]) * expert_pair[..., 1, :]).astype(jnp.bfloat16)
-    expert_term = jnp.einsum(
-        "secf,efd->secd", expert_act, expert_down, preferred_element_type=jnp.float32
-    )
-    expert_total = lax.psum_scatter(
-        expert_term.astype(jnp.bfloat16), "tensor", scatter_dimension=3, tiled=True
-    )
-    returned = lax.all_to_all(expert_total, "seq", split_axis=0, concat_axis=0, tiled=True)
-    picked = returned.reshape(experts * cap, width_local)[slot_index].reshape(
-        tok_dev, topk, width_local
-    )
-    mixture = jnp.sum(gates[..., None] * picked.astype(jnp.float32), 1)
+    slots = (
+        (slot_index // (exp_dev * cap)) * cap + slot_index % cap
+    ).reshape(tok_dev, topk)
+    member = (expert_ids % exp_dev).reshape(tok_dev, topk)
+    mixture = 0.0
+    for local in range(exp_dev):
+        here = (slots[:, :, None] == lax.iota(jnp.int32, seq_count * cap)[None, None, :]) & (
+            member[:, :, None] == local
+        )
+        placement = jnp.any(here, 1).astype(jnp.bfloat16)
+        outgoing = lax.dot_general(
+            placement, normed, (((0,), (0,)), ((), ())), preferred_element_type=jnp.float32
+        ).astype(jnp.bfloat16)
+        incoming = lax.all_to_all(
+            outgoing.reshape(seq_count, cap, width_local),
+            "seq",
+            split_axis=0,
+            concat_axis=0,
+            tiled=True,
+        ).reshape(seq_count * cap, width_local)
+        routed_rows = lax.all_gather(incoming, "tensor", axis=1, tiled=True)
+        expert_pair = jnp.einsum(
+            "rd,djf->rjf",
+            routed_rows,
+            expert_gate_up[local],
+            preferred_element_type=jnp.float32,
+        )
+        expert_act = (jax.nn.silu(expert_pair[:, 0]) * expert_pair[:, 1]).astype(jnp.bfloat16)
+        expert_term = jnp.dot(
+            expert_act, expert_down[local], preferred_element_type=jnp.float32
+        )
+        expert_total = lax.psum_scatter(
+            expert_term.astype(jnp.bfloat16), "tensor", scatter_dimension=1, tiled=True
+        )
+        returned = lax.all_to_all(
+            expert_total.reshape(seq_count, cap, width_local),
+            "seq",
+            split_axis=0,
+            concat_axis=0,
+            tiled=True,
+        ).reshape(seq_count * cap, width_local)
+        portions = jnp.sum(jnp.where(here, gates[:, :, None], 0.0), 1)
+        high = portions.astype(jnp.bfloat16)
+        low = (portions - high.astype(jnp.float32)).astype(jnp.bfloat16)
+        mixture += jnp.dot(high, returned, preferred_element_type=jnp.float32) + jnp.dot(
+            low, returned, preferred_element_type=jnp.float32
+        )
     return (stream + shared_out + mixture).astype(jnp.bfloat16)
 
 

time: 455 us -> 381 us (0.84)
  waiting for transfers between devices: 250 us -> 119 us
  Pallas kernels: 30.3 us -> 74.2 us
  local copies, waits for them, and re-layouts: 36.1 us -> 16.8 us
  matrix products: 26.2 us -> 44.9 us
  starting transfers between devices: 25.5 us -> 36.1 us
  blocking collectives: 62.4 us -> 69.1 us
  other arithmetic: 10.5 us -> 5.51 us
    all_gather x2, waiting for transfers between devices: 93.2 us -> 0.04 us  [shards(): routed_rows = lax.all_gather(incoming, 'tensor', axis=1, tiled=True)]
    pallas_call x0 -> x1, Pallas kernels: none -> 43 us  [gather_rows(): pl.pallas_call(gather_kernel, in_specs=[pl.BlockSpec(memory_space=pl.ANY)...]
    all_to_all x1 -> x2, waiting for transfers between devices: 103 us -> 78.1 us  [shards(): lax.all_to_all(partials, 'seq', split_axis=0, concat_axis=0, tiled=True)]
    dot_general x3 -> x12, matrix products: 20.2 us -> 38.9 us  [the longest x2 11.8 us: shards(): jnp.einsum('rd,djf->rjf', routed_rows, expert_gate_up[local], preferred_e...]
    gather x2 -> x0, local copies, waits for them, and re-layouts: 11.8 us -> none  [the longest x1 6.42 us: shards(): returned.reshape(experts * cap, width_local)[slot_index]]
    reduce_scatter x1 -> x2, waiting for transfers between devices: 13.5 us -> 6.38 us  [shards(): lax.psum_scatter(expert_term.astype(jnp.bfloat16), 'tensor', scatter_dime...]
    all_to_all x1 -> x2, blocking collectives: 55.1 us -> 62 us  [shards(): lax.all_to_all(outgoing.reshape(seq_count, cap, width_local), 'seq', spli...]
    all_to_all x1 -> x2, waiting for transfers between devices: 37.3 us -> 30.4 us  [shards(): lax.all_to_all(expert_total.reshape(seq_count, cap, width_local), 'seq',...]
  transfers between devices with their start and end apart: 7 -> 10, of which waited for: 6 -> 7; matrix products, arithmetic and copies ran while one was open for 6% -> 11% of each run, Pallas kernels for 0% -> 4%
where the time goes in v2:
time: 381 us; the launch traced here: 379 us
  waiting for transfers between devices  119 us (31%)
  Pallas kernels  74.2 us (19%)
  blocking collectives  69.1 us (18%)
  matrix products  44.9 us (12%)
  starting transfers between devices  36.1 us (9%)
  local copies, waits for them, and re-layouts  16.8 us (4%)
  between operations  13.8 us (4%)
  other arithmetic  5.51 us (1%)
    all_to_all x2, waiting for transfers between devices, shards(): lax.all_to_all(partials, 'seq', split_axis=0, concat_axis=0, tiled=True)  78.1 us
    all_to_all x2, blocking collectives, shards(): lax.all_to_all(outgoing.reshape(seq_count, cap, width_local), 'seq', spli...  62 us
    pallas_call x1, Pallas kernels, gather_rows(): pl.pallas_call(gather_kernel, in_specs=[pl.BlockSpec(memory_space=pl.ANY)...  43 us
    all_to_all x2, waiting for transfers between devices, shards(): lax.all_to_all(expert_total.reshape(seq_count, cap, width_local), 'seq',...  30.4 us
    pallas_call x2, Pallas kernels, attention(): pl.pallas_call(lambda *refs: attention_kernel(tok_dev, *refs), grid_spec=...  23.4 us
    all_to_all x2, starting transfers between devices, shards(): lax.all_to_all(partials, 'seq', split_axis=0, concat_axis=0, tiled=True)  23.1 us
    unnamed x33, local copies, waits for them, and re-layouts  16.1 us
    all_to_all x2, starting transfers between devices, shards(): lax.all_to_all(expert_total.reshape(seq_count, cap, width_local), 'seq',...  12.5 us
  transfers between devices with their start and end apart: 10, of which 7 were waited for; matrix products, arithmetic and copies ran while one was open for 11% of the time, Pallas kernels for 4%

profile of v2, /device:TPU:12, one launch (start us, length us, event | category | flops | bytes accessed | tf_op | source)
XLA Modules:
  0.0 379.5 jit_solution(772089230131031696)
XLA Ops:
  6.5 43.0 %gather_rows.1.refs_1_ = bf16[2048,1024]{1,0:T(8,128)(2,1)} custom-call(bf16[128,1024]{1,0:T(8,128)(2,1)} %own_ref.1), custom_call_target="tpu_custom_call" | custom-call | tf_op jit(solution)/shard_map/gather_rows/pallas_call | solution.py:226
  51.8 2.2 copy-done.5
  54.0 2.2 copy-done.7
  56.2 11.6 %ragged_attention.2 = bf16[16,144,512]{2,1,0:T(8,128)(2,1)S(1)} custom-call(s32[4]{0:T(128)S(1)} %copy-done.11, bf16[2048,1024]{1,0:T(8,128)(2,1)S(1)} %copy-done.1, bf16[4,512,1024]{2,1,0:T(8,128)(2,1)S(1)} %copy-done.5, bf16[4,512,1024]{2,1,0:T(8,128)(2,1)S(1)} %copy-done.7, bf16[128,1024]{1,0:T(8,128)(2,1)S(1)} %copy-done.9, bf16[128,1024]{1,0:T(8,128)(2,1)S(1)} %copy-done.10), custom_call_target="tpu_custom_call" | custom-call | flops 8589934592 | bytes 16777216 | tf_op jit(solution)/shard_map/ragged_attention/pallas_call | solution.py:103
  69.3 18.3 %all-to-all-start = ((bf16[16,144,512]{2,1,0:T(8,128)(2,1)}), bf16[16,144,512]{2,1,0:T(8,128)(2,1)}, u32[]{:S(2)}, u32[]{:S(2)}) async-start(bf16[16,144,512]{2,1,0:T(8,128)(2,1)} %copy-done.4), calls=%async_computation | async-start | bytes 4718592 | tf_op jit(solution)/shard_map/all_to_all | solution.py:311
  94.2 11.7 %ragged_attention.3 = bf16[16,144,512]{2,1,0:T(8,128)(2,1)S(1)} custom-call(s32[4]{0:T(128)S(1)} %copy-done.11, bf16[2048,1024]{1,0:T(8,128)(2,1)S(1)} %copy-done.2, bf16[4,512,1024]{2,1,0:T(8,128)(2,1)S(1)} %copy-done.6, bf16[4,512,1024]{2,1,0:T(8,128)(2,1)S(1)} %copy-done.8, bf16[128,1024]{1,0:T(8,128)(2,1)S(1)} %copy-done.9, bf16[128,1024]{1,0:T(8,128)(2,1)S(1)} %copy-done.10), custom_call_target="tpu_custom_call" | custom-call | flops 8589934592 | bytes 16777216 | tf_op jit(solution)/shard_map/ragged_attention/pallas_call | solution.py:103
  107.3 32.3 %all-to-all-done.parts_ref = bf16[16,144,512]{2,1,0:T(8,128)(2,1)} async-done(((bf16[16,144,512]{2,1,0:T(8,128)(2,1)}), bf16[16,144,512]{2,1,0:T(8,128)(2,1)}, u32[]{:S(2)}, u32[]{:S(2)}) %all-to-all-start) | async-done | bytes 2359328 | tf_op jit(solution)/shard_map/all_to_all | solution.py:311
  139.6 4.9 %all-to-all-start.1 = ((bf16[16,144,512]{2,1,0:T(8,128)(2,1)}), bf16[16,144,512]{2,1,0:T(8,128)(2,1)}, u32[]{:S(2)}, u32[]{:S(2)}) async-start(bf16[16,144,512]{2,1,0:T(8,128)(2,1)} %copy-done.3), calls=%async_computation.1 | async-start | bytes 4718592 | tf_op jit(solution)/shard_map/all_to_all | solution.py:311
  144.9 3.8 %combine_blocks.2 = bf16[128,512]{1,0:T(8,128)(2,1)S(1)} custom-call(bf16[16,144,512]{2,1,0:T(8,128)(2,1)} %all-to-all-done.parts_ref), custom_call_target="tpu_custom_call" | custom-call | tf_op jit(solution)/shard_map/combine_blocks/pallas_call | solution.py:259
  148.8 3.0 fusion.14
  151.8 45.8 %all-to-all-done.1.parts_ref = bf16[16,144,512]{2,1,0:T(8,128)(2,1)} async-done(((bf16[16,144,512]{2,1,0:T(8,128)(2,1)}), bf16[16,144,512]{2,1,0:T(8,128)(2,1)}, u32[]{:S(2)}, u32[]{:S(2)}) %all-to-all-start.1) | async-done | bytes 2359328 | tf_op jit(solution)/shard_map/all_to_all | solution.py:311
  197.6 3.9 %combine_blocks.3 = bf16[128,512]{1,0:T(8,128)(2,1)S(1)} custom-call(bf16[16,144,512]{2,1,0:T(8,128)(2,1)} %all-to-all-done.1.parts_ref), custom_call_target="tpu_custom_call" | custom-call | tf_op jit(solution)/shard_map/combine_blocks/pallas_call | solution.py:259
  201.5 2.9 fusion.10
  207.5 4.0 %reduce-scatter.5.cloned.1.call-done = bf16[128,1024]{1,0:T(8,128)(2,1)} async-done(((bf16[128,2048]{1,0:T(8,128)(2,1)}), bf16[128,1024]{1,0:T(8,128)(2,1)}) %reduce-scatter.5.cloned.1.call-update) | async-done | bytes 262160 | tf_op jit(solution)/shard_map/reduce_scatter | solution.py:317
  212.6 2.5 psum.14
  216.6 32.5 %all_to_all.30 = bf16[16,32,1024]{2,1,0:T(8,128)(2,1)} all-to-all(bf16[16,32,1024]{2,1,0:T(8,128)(2,1)S(1)} %bitcast.83), channel_id=1, replica_groups=mesh['seq'=16,'tensor'=2] {'seq'}, dimensions={0} | all-to-all | bytes 2097152 | tf_op jit(solution)/shard_map/all_to_all | solution.py:361
  249.7 29.5 %all_to_all.31 = bf16[16,32,1024]{2,1,0:T(8,128)(2,1)} all-to-all(bf16[16,32,1024]{2,1,0:T(8,128)(2,1)S(1)} %bitcast.84), channel_id=1, replica_groups=mesh['seq'=16,'tensor'=2] {'seq'}, dimensions={0} | all-to-all | bytes 2097152 | tf_op jit(solution)/shard_map/all_to_all | solution.py:361
  279.5 5.9 %fusion = f32[512,2,704]{0,2,1:T(8,128)S(1)} fusion(bf16[2,2048,2,704]{1,3,2,0:T(8,128)(2,1)} %param.26, bf16[512,2048]{1,0:T(8,128)(2,1)} %all-gather.5.cloned.1.call-done), kind=kOutput, calls=%fused_computation | convolution fusion | flops 2952790016 | bytes 10747904 | tf_op jit(solution)/shard_map/rd,djf->rjf/dot_general | solution.py:369
  285.4 5.3 %convolution_convert_fusion = bf16[512,2048]{1,0:T(8,128)(2,1)} fusion(bf16[2,704,2048]{2,1,0:T(8,128)(2,1)} %param.27, f32[512,2,704]{0,2,1:T(8,128)S(1)} %fusion), kind=kOutput, calls=%fused_computation.6 | convolution fusion | flops 1479606272 | bytes 7864320 | tf_op jit(solution)/shard_map/dot_general | solution.py:376
  290.8 5.9 %fusion.2 = f32[512,2,704]{0,2,1:T(8,128)S(1)} fusion(bf16[2,2048,2,704]{1,3,2,0:T(8,128)(2,1)} %param.26, bf16[512,2048]{1,0:T(8,128)(2,1)} %all-gather.3.cloned.1.call-done), kind=kOutput, calls=%fused_computation.2 | convolution fusion | flops 2952790016 | bytes 10747904 | tf_op jit(solution)/shard_map/rd,djf->rjf/dot_general | solution.py:369
  296.7 5.1 %convolution_convert_fusion.1 = bf16[512,2048]{1,0:T(8,128)(2,1)} fusion(bf16[2,704,2048]{2,1,0:T(8,128)(2,1)} %param.27, f32[512,2,704]{0,2,1:T(8,128)S(1)} %fusion.2), kind=kOutput, calls=%fused_computation.7 | convolution fusion | flops 1479606272 | bytes 7864320 | tf_op jit(solution)/shard_map/dot_general | solution.py:376
  302.2 7.0 %all-to-all-start.5 = ((bf16[16,32,1024]{2,1,0:T(8,128)(2,1)}), bf16[16,32,1024]{2,1,0:T(8,128)(2,1)}, u32[]{:S(2)}, u32[]{:S(2)}) async-start(bf16[16,32,1024]{2,1,0:T(8,128)(2,1)} %bitcast.86), calls=%async_computation.9 | async-start | bytes 2097152 | tf_op jit(solution)/shard_map/all_to_all | solution.py:382
  309.2 6.0 %reduce-scatter.9.cloned.1.call-done = bf16[512,1024]{1,0:T(8,128)(2,1)} async-done(((bf16[512,2048]{1,0:T(8,128)(2,1)}), bf16[512,1024]{1,0:T(8,128)(2,1)}) %reduce-scatter.9.cloned.1.call-update) | async-done | bytes 1048592 | tf_op jit(solution)/shard_map/reduce_scatter | solution.py:379
  315.2 19.8 %all-to-all-done.5 = bf16[16,32,1024]{2,1,0:T(8,128)(2,1)} async-done(((bf16[16,32,1024]{2,1,0:T(8,128)(2,1)}), bf16[16,32,1024]{2,1,0:T(8,128)(2,1)}, u32[]{:S(2)}, u32[]{:S(2)}) %all-to-all-start.5) | async-done | bytes 1048608 | tf_op jit(solution)/shard_map/all_to_all | solution.py:382
  335.0 5.5 %all-to-all-start.3 = ((bf16[16,32,1024]{2,1,0:T(8,128)(2,1)}), bf16[16,32,1024]{2,1,0:T(8,128)(2,1)}, u32[]{:S(2)}, u32[]{:S(2)}) async-start(bf16[16,32,1024]{2,1,0:T(8,128)(2,1)} %bitcast.85), calls=%async_computation.6 | async-start | bytes 2097152 | tf_op jit(solution)/shard_map/all_to_all | solution.py:382
  340.8 2.5 psum.15
  345.5 4.3 %fusion.29 = f32[128,2,704]{0,2,1:T(8,128)S(1)} fusion(bf16[2048,2,704]{0,2,1:T(8,128)(2,1)} %param.28, bf16[128,2048]{1,0:T(8,128)(2,1)S(1)} %all_gather.9), kind=kOutput, calls=%fused_computation.41 | convolution fusion | flops 738197504 | bytes 7012352 | tf_op jit(solution)/shard_map/td,dcf->tcf/dot_general | solution.py:332
  352.1 2.3 fusion.40
  354.4 10.6 %all-to-all-done.3 = bf16[16,32,1024]{2,1,0:T(8,128)(2,1)} async-done(((bf16[16,32,1024]{2,1,0:T(8,128)(2,1)}), bf16[16,32,1024]{2,1,0:T(8,128)(2,1)}, u32[]{:S(2)}, u32[]{:S(2)}) %all-to-all-start.3) | async-done | bytes 1048608 | tf_op jit(solution)/shard_map/all_to_all | solution.py:382
  365.0 2.4 fusion.43
  367.4 2.5 convolution_add_fusion.1
  369.9 2.8 fusion.24
  (72 shorter events, 23.8 us)
Async XLA Ops:
  6.5 343.3 %copy-start = (bf16[704,2048]{1,0:T(8,128)(2,1)S(1)}, bf16[704,2048]{1,0:T(8,128)(2,1)}, u32[]{:S(2)}) copy-start(bf16[704,2048]{1,0:T(8,128)(2,1)} %param.29) | copy-start | bytes 8650756
  6.5 43.1 %copy-start.9 = (bf16[128,1024]{1,0:T(8,128)(2,1)S(1)}, bf16[128,1024]{1,0:T(8,128)(2,1)}, u32[]{:S(2)}) copy-start(bf16[128,1024]{1,0:T(8,128)(2,1)} %refs_4_.3) | copy-start | bytes 786436
  6.5 43.1 %copy-start.10 = (bf16[128,1024]{1,0:T(8,128)(2,1)S(1)}, bf16[128,1024]{1,0:T(8,128)(2,1)}, u32[]{:S(2)}) copy-start(bf16[128,1024]{1,0:T(8,128)(2,1)} %refs_5_.3) | copy-start | bytes 786436
  6.5 43.1 %copy-start.11 = (s32[4]{0:T(128)S(1)}, s32[4]{0:T(128)}, u32[]{:S(2)}) copy-start(s32[4]{0:T(128)} %refs_0_.3) | copy-start | bytes 52
  49.6 2.2 copy-start.1
  51.8 2.2 copy-start.5
  54.0 2.2 copy-start.7
  67.8 1.5 copy-start.4
  69.3 70.3 %all-to-all-start = ((bf16[16,144,512]{2,1,0:T(8,128)(2,1)}), bf16[16,144,512]{2,1,0:T(8,128)(2,1)}, u32[]{:S(2)}, u32[]{:S(2)}) async-start(bf16[16,144,512]{2,1,0:T(8,128)(2,1)} %copy-done.4), calls=%async_computation | async-start | bytes 4718592 | tf_op jit(solution)/shard_map/all_to_all | solution.py:311
  87.6 2.2 copy-start.2
  89.8 2.2 copy-start.6
  92.0 2.2 copy-start.8
  105.9 1.4 copy-start.3
  107.3 37.2 %copy-start.14 = (s32[128,6]{0,1:T(8,128)S(1)}, s32[128,6]{0,1:T(8,128)}, u32[]{:S(2)}) copy-start(s32[128,6]{0,1:T(8,128)} %param.25) | copy-start | bytes 9220
  139.6 57.9 %all-to-all-start.1 = ((bf16[16,144,512]{2,1,0:T(8,128)(2,1)}), bf16[16,144,512]{2,1,0:T(8,128)(2,1)}, u32[]{:S(2)}, u32[]{:S(2)}) async-start(bf16[16,144,512]{2,1,0:T(8,128)(2,1)} %copy-done.3), calls=%async_computation.1 | async-start | bytes 4718592 | tf_op jit(solution)/shard_map/all_to_all | solution.py:311
  144.5 67.0 %reduce-scatter.5.cloned.1.call-start = ((), (), s32[]{:S(2)}) async-start(), calls=%async_computation.10 | async-start | bytes 786432 | tf_op jit(solution)/shard_map/reduce_scatter | solution.py:317
  197.6 3.9 %copy-start.12 = (f32[128,2048]{1,0:T(8,128)S(1)}, f32[128,2048]{1,0:T(8,128)}, u32[]{:S(2)}) copy-start(f32[128,2048]{1,0:T(8,128)} %fusion.14) | copy-start | bytes 3145732
  201.5 9.9 %copy-start.13 = (bf16[128,1024]{1,0:T(8,128)(2,1)S(1)}, bf16[128,1024]{1,0:T(8,128)(2,1)}, u32[]{:S(2)}) copy-start(bf16[128,1024]{1,0:T(8,128)(2,1)} %param.15) | copy-start | bytes 786436
  204.4 75.0 %all-gather.5.cloned.1.call-start = ((), (), s32[]{:S(2)}) async-start(), calls=%async_computation.14 | async-start | bytes 3145728 | tf_op jit(solution)/shard_map/all_gather | solution.py:368
  249.1 41.6 %all-gather.3.cloned.1.call-start = ((), (), s32[]{:S(2)}) async-start(), calls=%async_computation.12 | async-start | bytes 3145728 | tf_op jit(solution)/shard_map/all_gather | solution.py:368
  279.2 23.0 %reduce-scatter.11.cloned.1.call-start = ((), (), s32[]{:S(2)}) async-start(), calls=%async_computation.15 | async-start | bytes 3145728 | tf_op jit(solution)/shard_map/reduce_scatter | solution.py:379
  290.7 24.5 %reduce-scatter.9.cloned.1.call-start = ((), (), s32[]{:S(2)}) async-start(), calls=%async_computation.13 | async-start | bytes 3145728 | tf_op jit(solution)/shard_map/reduce_scatter | solution.py:379
  301.8 38.8 %copy-start.15 = (bf16[1024,32]{0,1:T(8,128)(2,1)S(1)}, bf16[1024,32]{0,1:T(8,128)(2,1)}, u32[]{:S(2)}) copy-start(bf16[1024,32]{0,1:T(8,128)(2,1)} %param.24) | copy-start | bytes 196612
  302.2 32.8 %all-to-all-start.5 = ((bf16[16,32,1024]{2,1,0:T(8,128)(2,1)}), bf16[16,32,1024]{2,1,0:T(8,128)(2,1)}, u32[]{:S(2)}, u32[]{:S(2)}) async-start(bf16[16,32,1024]{2,1,0:T(8,128)(2,1)} %bitcast.86), calls=%async_computation.9 | async-start | bytes 2097152 | tf_op jit(solution)/shard_map/all_to_all | solution.py:382
  335.0 30.0 %all-to-all-start.3 = ((bf16[16,32,1024]{2,1,0:T(8,128)(2,1)}), bf16[16,32,1024]{2,1,0:T(8,128)(2,1)}, u32[]{:S(2)}, u32[]{:S(2)}) async-start(bf16[16,32,1024]{2,1,0:T(8,128)(2,1)} %bitcast.85), calls=%async_computation.6 | async-start | bytes 2097152 | tf_op jit(solution)/shard_map/all_to_all | solution.py:382
  340.5 29.3 %reduce-scatter.7.cloned.1.call-start = ((), (), s32[]{:S(2)}) async-start(), calls=%async_computation.11 | async-start | bytes 786432 | tf_op jit(solution)/shard_map/reduce_scatter | solution.py:337
Sparse Core Ops, SparseCore 0:
  204.6 6.8 reduce-scatter.4
  249.3 9.8 all-gather.4
  279.3 9.8 all-gather.2
  291.4 10.7 reduce-scatter.10
  304.3 10.7 reduce-scatter.8
  351.4 9.0 reduce-scatter.6

commit v3 on v2

--- a/solution.py
+++ b/solution.py
@@ -63,27 +63,29 @@
     def rounded(top):
         return top.astype(jnp.bfloat16).astype(jnp.float32)
 
-    visible = lax.broadcasted_iota(jnp.int32, (clen_dev, rows), 0) < remaining
+    floor = 0.1 * negative
+    hidden = jnp.where(
+        lax.broadcasted_iota(jnp.int32, (clen_dev, 1), 0) < remaining, 0.0, negative
+    )
 
     @pl.when(own)
     def _():
-        cached = jnp.where(visible, scored(k_ref[0]), negative)
+        cached = scored(k_ref[0]) + hidden
         place = lax.broadcasted_iota(jnp.int32, (tok_dev, rows), 0) + own_start % rows
         seen = place <= lax.broadcasted_iota(jnp.int32, (tok_dev, rows), 1)
         fresh = jnp.where(seen, scored(nk_ref[...]), negative)
-        top = rounded(
-            jnp.maximum(jnp.max(cached, 0, keepdims=True), jnp.max(fresh, 0, keepdims=True))
-        )
-        cached = jnp.where(visible, jnp.exp2(cached - top), 0.0)
-        fresh = jnp.where(seen, jnp.exp2(fresh - top), 0.0)
+        top = jnp.maximum(jnp.max(cached, 0, keepdims=True), jnp.max(fresh, 0, keepdims=True))
+        top = rounded(jnp.maximum(top, floor))
+        cached = jnp.exp2(cached - top)
+        fresh = jnp.exp2(fresh - top)
         total = jnp.sum(cached, 0, keepdims=True) + jnp.sum(fresh, 0, keepdims=True)
         emit(weighted(cached, v_ref[0]) + weighted(fresh, nv_ref[...]), top, total)
 
     @pl.when(jnp.logical_not(own) & (remaining > 0))
     def _():
-        cached = jnp.where(visible, scored(k_ref[0]), negative)
+        cached = scored(k_ref[0]) + hidden
         top = rounded(jnp.max(cached, 0, keepdims=True))
-        cached = jnp.where(visible, jnp.exp2(cached - top), 0.0)
+        cached = jnp.exp2(cached - top)
         emit(weighted(cached, v_ref[0]), top, jnp.sum(cached, 0, keepdims=True))
 
     @pl.when(jnp.logical_not(own) & (remaining <= 0))
@@ -119,7 +121,7 @@
         out_shape=jax.ShapeDtypeStruct(
             (tokens // tok_dev, tok_dev + STAT_ROWS, heads * HD), jnp.bfloat16
         ),
-        compiler_params=pltpu.CompilerParams(vmem_limit_bytes=32 * 1024 * 1024),
+        compiler_params=pltpu.CompilerParams(vmem_limit_bytes=56 * 1024 * 1024),
         cost_estimate=pl.CostEstimate(
             flops=4 * requests * NEW * clen_dev * heads * HD * 4,
             bytes_accessed=16 * 1024 * 1024,
@@ -229,7 +231,9 @@
         out_specs=pl.BlockSpec(memory_space=pl.ANY),
         out_shape=jax.ShapeDtypeStruct((rows.shape[0] * count, rows.shape[1]), rows.dtype),
         scratch_shapes=[pltpu.SemaphoreType.DMA] + [pltpu.SemaphoreType.DMA((planes,))] * 10,
-        compiler_params=pltpu.CompilerParams(collective_id=0, has_side_effects=True),
+        compiler_params=pltpu.CompilerParams(
+            collective_id=0, has_side_effects=True, vmem_limit_bytes=56 * 1024 * 1024
+        ),
         name="gather_rows",
     )(rows)
 
@@ -293,12 +297,13 @@
     topk = expert_ids.shape[1]
     every_query = gather_rows(queries, seq_count)
     heads_local = queries.shape[1] // HD
-    pieces = 2 if heads_local % 2 == 0 else 1
-    heads_piece = heads_local // pieces
+    early = max(heads_local // 4, 1)
     projected = 0.0
-    for piece in range(pieces):
+    for first, heads_piece in ((0, early), (early, heads_local - early)):
+        if heads_piece == 0:
+            continue
         partials = attention(
-            piece * heads_piece,
+            first,
             heads_piece,
             cache_lengths,
             every_query,
@@ -310,7 +315,7 @@
         attended = combine(
             lax.all_to_all(partials, "seq", split_axis=0, concat_axis=0, tiled=True)
         )
-        features = slice(piece * heads_piece * HD, (piece + 1) * heads_piece * HD)
+        features = slice(first * HD, (first + heads_piece) * HD)
         projected += jnp.dot(
             attended, out_proj[features], preferred_element_type=jnp.float32
         )
@@ -350,14 +355,19 @@
     ).reshape(tok_dev, topk)
     member = (expert_ids % exp_dev).reshape(tok_dev, topk)
     mixture = 0.0
-    for local in range(exp_dev):
-        here = (slots[:, :, None] == lax.iota(jnp.int32, seq_count * cap)[None, None, :]) & (
-            member[:, :, None] == local
-        )
-        placement = jnp.any(here, 1).astype(jnp.bfloat16)
+    places = [
+        (slots[:, :, None] == lax.iota(jnp.int32, seq_count * cap)[None, None, :])
+        & (member[:, :, None] == local)
+        for local in range(exp_dev)
+    ]
+
+    def received(local, after):
+        placement = jnp.any(places[local], 1).astype(jnp.bfloat16)
         outgoing = lax.dot_general(
             placement, normed, (((0,), (0,)), ((), ())), preferred_element_type=jnp.float32
         ).astype(jnp.bfloat16)
+        if after is not None:
+            outgoing, after = lax.optimization_barrier((outgoing, after))
         incoming = lax.all_to_all(
             outgoing.reshape(seq_count, cap, width_local),
             "seq",
@@ -365,6 +375,14 @@
             concat_axis=0,
             tiled=True,
         ).reshape(seq_count * cap, width_local)
+        return incoming, after
+
+    pairs = []
+    incoming, _ = received(0, None)
+    for local in range(exp_dev):
+        following = None
+        if local + 1 < exp_dev:
+            following, incoming = received(local + 1, incoming)
         routed_rows = lax.all_gather(incoming, "tensor", axis=1, tiled=True)
         expert_pair = jnp.einsum(
             "rd,djf->rjf",
@@ -372,6 +390,11 @@
             expert_gate_up[local],
             preferred_element_type=jnp.float32,
         )
+        if following is not None:
+            incoming, expert_pair = lax.optimization_barrier((following, expert_pair))
+        pairs.append(expert_pair)
+    for local in range(exp_dev):
+        here, expert_pair = places[local], pairs[local]
         expert_act = (jax.nn.silu(expert_pair[:, 0]) * expert_pair[:, 1]).astype(jnp.bfloat16)
         expert_term = jnp.dot(
             expert_act, expert_down[local], preferred_element_type=jnp.float32

time: 381 us -> 367 us (0.963)
  blocking collectives: 69.1 us -> 39.8 us
  waiting for transfers between devices: 119 us -> 138 us
  local copies, waits for them, and re-layouts: 16.8 us -> 0.84 us
  Pallas kernels: 74.2 us -> 81.9 us
    all_to_all x0 -> x2, waiting for transfers between devices: none -> 35.9 us  [received(): lax.all_to_all(outgoing.reshape(seq_count, cap, width_local), 'seq', spli...]
    all_to_all x2 -> x1, blocking collectives: 62 us -> 32.7 us  [shards(): lax.all_to_all(expert_total.reshape(seq_count, cap, width_local), 'seq',...]
    all_to_all x2 -> x1, waiting for transfers between devices: 30.4 us -> 10.7 us  [shards(): lax.all_to_all(expert_total.reshape(seq_count, cap, width_local), 'seq',...]
    unnamed x33 -> x11, local copies, waits for them, and re-layouts: 16.1 us -> 0.13 us
    all_to_all x0 -> x2, starting transfers between devices: none -> 12.6 us  [received(): lax.all_to_all(outgoing.reshape(seq_count, cap, width_local), 'seq', spli...]
    all_gather x2, waiting for transfers between devices: 0.04 us -> 8.5 us  [shards(): routed_rows = lax.all_gather(incoming, 'tensor', axis=1, tiled=True)]
    pallas_call x2, Pallas kernels: 23.4 us -> 31.1 us  [attention(): pl.pallas_call(lambda *refs: attention_kernel(tok_dev, *refs), grid_spec=...]
    all_to_all x2 -> x1, starting transfers between devices: 12.5 us -> 5.28 us  [shards(): lax.all_to_all(expert_total.reshape(seq_count, cap, width_local), 'seq',...]
  transfers between devices with their start and end apart: 10 -> 11, of which waited for: 7 -> 9; matrix products, arithmetic and copies ran while one was open for 11% -> 12% of each run, Pallas kernels for 4% -> 7%
where the time goes in v3:
time: 367 us; the launch traced here: 364 us
  waiting for transfers between devices  138 us (38%)
  Pallas kernels  81.9 us (22%)
  matrix products  48.7 us (13%)
  blocking collectives  39.8 us (11%)
  starting transfers between devices  36.3 us (10%)
  between operations  13.7 us (4%)
  other arithmetic  5.51 us (2%)
    all_to_all x2, waiting for transfers between devices, shards(): lax.all_to_all(partials, 'seq', split_axis=0, concat_axis=0, tiled=True)  76.3 us
    pallas_call x1, Pallas kernels, gather_rows(): pl.pallas_call(gather_kernel, in_specs=[pl.BlockSpec(memory_space=pl.ANY)...  43 us
    all_to_all x2, waiting for transfers between devices, received(): lax.all_to_all(outgoing.reshape(seq_count, cap, width_local), 'seq', spli...  35.9 us
    all_to_all x1, blocking collectives, shards(): lax.all_to_all(expert_total.reshape(seq_count, cap, width_local), 'seq',...  32.7 us
    pallas_call x2, Pallas kernels, attention(): pl.pallas_call(lambda *refs: attention_kernel(tok_dev, *refs), grid_spec=...  31.1 us
    all_to_all x2, starting transfers between devices, shards(): lax.all_to_all(partials, 'seq', split_axis=0, concat_axis=0, tiled=True)  18 us
    dot_general x2, matrix products, shards(): jnp.einsum('rd,djf->rjf', routed_rows, expert_gate_up[local], preferred_e...  13.9 us
    all_to_all x2, starting transfers between devices, received(): lax.all_to_all(outgoing.reshape(seq_count, cap, width_local), 'seq', spli...  12.6 us
  transfers between devices with their start and end apart: 11, of which 9 were waited for; matrix products, arithmetic and copies ran while one was open for 12% of the time, Pallas kernels for 7%

profile of v3, /device:TPU:12, one launch (start us, length us, event | category | flops | bytes accessed | tf_op | source)
XLA Modules:
  0.0 364.4 jit_solution(10086554122635394423)
XLA Ops:
  6.5 43.0 %gather_rows.1.refs_1_ = bf16[2048,1024]{1,0:T(8,128)(2,1)} custom-call(bf16[128,1024]{1,0:T(8,128)(2,1)} %own_ref.1), custom_call_target="tpu_custom_call" | custom-call | tf_op jit(solution)/shard_map/gather_rows/pallas_call | solution.py:228
  49.5 9.0 %ragged_attention.2 = bf16[16,144,256]{2,1,0:T(8,128)(2,1)} custom-call(s32[4]{0:T(128)} %refs_0_.3, bf16[2048,1024]{1,0:T(8,128)(2,1)} %gather_rows.1.refs_1_, bf16[4,512,1024]{2,1,0:T(8,128)(2,1)} %refs_2_.3, bf16[4,512,1024]{2,1,0:T(8,128)(2,1)} %refs_3_.3, bf16[128,1024]{1,0:T(8,128)(2,1)} %refs_4_.3, bf16[128,1024]{1,0:T(8,128)(2,1)} %refs_5_.3), custom_call_target="tpu_custom_call" | custom-call | flops 4294967296 | bytes 16777216 | tf_op jit(solution)/shard_map/ragged_attention/pallas_call | solution.py:105
  58.5 13.1 %all-to-all-start = ((bf16[16,144,256]{2,1,0:T(8,128)(2,1)}), bf16[16,144,256]{2,1,0:T(8,128)(2,1)}, u32[]{:S(2)}, u32[]{:S(2)}) async-start(bf16[16,144,256]{2,1,0:T(8,128)(2,1)} %ragged_attention.2), calls=%async_computation | async-start | bytes 2359296 | tf_op jit(solution)/shard_map/all_to_all | solution.py:316
  71.6 22.1 %ragged_attention.3 = bf16[16,144,768]{2,1,0:T(8,128)(2,1)} custom-call(s32[4]{0:T(128)} %refs_0_.3, bf16[2048,1024]{1,0:T(8,128)(2,1)} %gather_rows.1.refs_1_, bf16[4,512,1024]{2,1,0:T(8,128)(2,1)} %refs_2_.3, bf16[4,512,1024]{2,1,0:T(8,128)(2,1)} %refs_3_.3, bf16[128,1024]{1,0:T(8,128)(2,1)} %refs_4_.3, bf16[128,1024]{1,0:T(8,128)(2,1)} %refs_5_.3), custom_call_target="tpu_custom_call" | custom-call | flops 12884901888 | bytes 16777216 | tf_op jit(solution)/shard_map/ragged_attention/pallas_call | solution.py:105
  93.7 4.3 %all-to-all-done.parts_ref = bf16[16,144,256]{2,1,0:T(8,128)(2,1)} async-done(((bf16[16,144,256]{2,1,0:T(8,128)(2,1)}), bf16[16,144,256]{2,1,0:T(8,128)(2,1)}, u32[]{:S(2)}, u32[]{:S(2)}) %all-to-all-start) | async-done | bytes 1179680 | tf_op jit(solution)/shard_map/all_to_all | solution.py:316
  98.0 5.0 %all-to-all-start.1 = ((bf16[16,144,768]{2,1,0:T(8,128)(2,1)}), bf16[16,144,768]{2,1,0:T(8,128)(2,1)}, u32[]{:S(2)}, u32[]{:S(2)}) async-start(bf16[16,144,768]{2,1,0:T(8,128)(2,1)} %ragged_attention.3), calls=%async_computation.1 | async-start | bytes 7077888 | tf_op jit(solution)/shard_map/all_to_all | solution.py:316
  103.4 2.2 combine_blocks.2
  105.6 2.6 fusion.28
  108.2 72.1 %all-to-all-done.1.parts_ref = bf16[16,144,768]{2,1,0:T(8,128)(2,1)} async-done(((bf16[16,144,768]{2,1,0:T(8,128)(2,1)}), bf16[16,144,768]{2,1,0:T(8,128)(2,1)}, u32[]{:S(2)}, u32[]{:S(2)}) %all-to-all-start.1) | async-done | bytes 3538976 | tf_op jit(solution)/shard_map/all_to_all | solution.py:316
  180.3 5.6 %combine_blocks.3 = bf16[128,768]{1,0:T(8,128)(2,1)S(1)} custom-call(bf16[16,144,768]{2,1,0:T(8,128)(2,1)} %all-to-all-done.1.parts_ref), custom_call_target="tpu_custom_call" | custom-call | tf_op jit(solution)/shard_map/combine_blocks/pallas_call | solution.py:263
  185.9 3.3 fusion.15
  192.2 4.2 %reduce-scatter.5.cloned.1.call-done = bf16[128,1024]{1,0:T(8,128)(2,1)} async-done(((bf16[128,2048]{1,0:T(8,128)(2,1)}), bf16[128,1024]{1,0:T(8,128)(2,1)}) %reduce-scatter.5.cloned.1.call-update) | async-done | bytes 262160 | tf_op jit(solution)/shard_map/reduce_scatter | solution.py:322
  197.5 2.5 psum.14
  202.6 7.0 %all-to-all-start.2 = ((bf16[16,32,1024]{2,1,0:T(8,128)(2,1)}), bf16[16,32,1024]{2,1,0:T(8,128)(2,1)}, u32[]{:S(2)}, u32[]{:S(2)}) async-start(bf16[16,32,1024]{2,1,0:T(8,128)(2,1)} %bitcast.84), calls=%async_computation.4 | async-start | bytes 2097152 | tf_op jit(solution)/shard_map/all_to_all | solution.py:371
  211.1 24.3 %all-to-all-done.2 = bf16[16,32,1024]{2,1,0:T(8,128)(2,1)} async-done(((bf16[16,32,1024]{2,1,0:T(8,128)(2,1)}), bf16[16,32,1024]{2,1,0:T(8,128)(2,1)}, u32[]{:S(2)}, u32[]{:S(2)}) %all-to-all-start.2) | async-done | bytes 1048608 | tf_op jit(solution)/shard_map/all_to_all | solution.py:371
  235.4 5.6 %all-to-all-start.3 = ((bf16[16,32,1024]{2,1,0:T(8,128)(2,1)}), bf16[16,32,1024]{2,1,0:T(8,128)(2,1)}, u32[]{:S(2)}, u32[]{:S(2)}) async-start(bf16[16,32,1024]{2,1,0:T(8,128)(2,1)} %bitcast.83), calls=%async_computation.5 | async-start | bytes 2097152 | tf_op jit(solution)/shard_map/all_to_all | solution.py:371
  241.0 4.9 %all-gather.3.cloned.1.call-done = bf16[512,2048]{1,0:T(8,128)(2,1)} async-done(((bf16[512,1024]{1,0:T(8,128)(2,1)}), bf16[512,2048]{1,0:T(8,128)(2,1)}) %all-gather.3.cloned.1.call-update) | async-done | bytes 2097168 | tf_op jit(solution)/shard_map/all_gather | solution.py:386
  245.9 8.0 %fusion.2 = f32[512,2,704]{0,2,1:T(8,128)} fusion(bf16[2,2048,2,704]{1,3,2,0:T(8,128)(2,1)} %param.26, bf16[512,2048]{1,0:T(8,128)(2,1)} %all-gather.3.cloned.1.call-done), kind=kOutput, calls=%fused_computation.2 | convolution fusion | flops 2952790016 | bytes 10747904 | tf_op jit(solution)/shard_map/rd,djf->rjf/dot_general | solution.py:387
  254.0 11.6 %all-to-all-done.3 = bf16[16,32,1024]{2,1,0:T(8,128)(2,1)} async-done(((bf16[16,32,1024]{2,1,0:T(8,128)(2,1)}), bf16[16,32,1024]{2,1,0:T(8,128)(2,1)}, u32[]{:S(2)}, u32[]{:S(2)}) %all-to-all-start.3) | async-done | bytes 1048608 | tf_op jit(solution)/shard_map/all_to_all | solution.py:371
  265.8 5.9 %convolution_convert_fusion.1 = bf16[512,2048]{1,0:T(8,128)(2,1)} fusion(bf16[2,704,2048]{2,1,0:T(8,128)(2,1)} %param.27, f32[512,2,704]{0,2,1:T(8,128)} %fusion.2), kind=kOutput, calls=%fused_computation.9 | convolution fusion | flops 1479606272 | bytes 7864320 | tf_op jit(solution)/shard_map/dot_general | solution.py:399
  271.8 3.6 all-gather.5.cloned.1.call-done
  275.4 5.9 %fusion = f32[512,2,704]{0,2,1:T(8,128)S(1)} fusion(bf16[2,2048,2,704]{1,3,2,0:T(8,128)(2,1)} %param.26, bf16[512,2048]{1,0:T(8,128)(2,1)} %all-gather.5.cloned.1.call-done), kind=kOutput, calls=%fused_computation | convolution fusion | flops 2952790016 | bytes 10747904 | tf_op jit(solution)/shard_map/rd,djf->rjf/dot_general | solution.py:387
  281.3 5.1 %convolution_convert_fusion = bf16[512,2048]{1,0:T(8,128)(2,1)} fusion(bf16[2,704,2048]{2,1,0:T(8,128)(2,1)} %param.27, f32[512,2,704]{0,2,1:T(8,128)S(1)} %fusion), kind=kOutput, calls=%fused_computation.8 | convolution fusion | flops 1479606272 | bytes 7864320 | tf_op jit(solution)/shard_map/dot_general | solution.py:399
  288.4 32.7 %all_to_all.30 = bf16[16,32,1024]{2,1,0:T(8,128)(2,1)} all-to-all(bf16[16,32,1024]{2,1,0:T(8,128)(2,1)} %bitcast.86), channel_id=1, replica_groups=mesh['seq'=16,'tensor'=2] {'seq'}, dimensions={0} | all-to-all | bytes 2097152 | tf_op jit(solution)/shard_map/all_to_all | solution.py:405
  321.1 5.3 %all-to-all-start.5 = ((bf16[16,32,1024]{2,1,0:T(8,128)(2,1)}), bf16[16,32,1024]{2,1,0:T(8,128)(2,1)}, u32[]{:S(2)}, u32[]{:S(2)}) async-start(bf16[16,32,1024]{2,1,0:T(8,128)(2,1)} %bitcast.85), calls=%async_computation.9 | async-start | bytes 2097152 | tf_op jit(solution)/shard_map/all_to_all | solution.py:405
  326.6 2.5 psum.15
  329.1 2.2 all_gather.9
  331.3 4.3 %fusion.33 = f32[128,2,704]{0,2,1:T(8,128)S(1)} fusion(bf16[2048,2,704]{0,2,1:T(8,128)(2,1)} %param.28, bf16[128,2048]{1,0:T(8,128)(2,1)S(1)} %all_gather.9), kind=kOutput, calls=%fused_computation.41 | convolution fusion | flops 738197504 | bytes 7012352 | tf_op jit(solution)/shard_map/td,dcf->tcf/dot_general | solution.py:337
  338.0 2.3 fusion.47
  340.3 10.7 %all-to-all-done.5 = bf16[16,32,1024]{2,1,0:T(8,128)(2,1)} async-done(((bf16[16,32,1024]{2,1,0:T(8,128)(2,1)}), bf16[16,32,1024]{2,1,0:T(8,128)(2,1)}, u32[]{:S(2)}, u32[]{:S(2)}) %all-to-all-start.5) | async-done | bytes 1048608 | tf_op jit(solution)/shard_map/all_to_all | solution.py:405
  352.5 2.3 convolution_add_fusion
  354.8 2.8 fusion.27
  (51 shorter events, 15.0 us)
Async XLA Ops:
  6.5 329.1 %copy-start = (bf16[704,2048]{1,0:T(8,128)(2,1)S(1)}, bf16[704,2048]{1,0:T(8,128)(2,1)}, u32[]{:S(2)}) copy-start(bf16[704,2048]{1,0:T(8,128)(2,1)} %param.29) | copy-start | bytes 8650756
  58.5 39.5 %all-to-all-start = ((bf16[16,144,256]{2,1,0:T(8,128)(2,1)}), bf16[16,144,256]{2,1,0:T(8,128)(2,1)}, u32[]{:S(2)}, u32[]{:S(2)}) async-start(bf16[16,144,256]{2,1,0:T(8,128)(2,1)} %ragged_attention.2), calls=%async_computation | async-start | bytes 2359296 | tf_op jit(solution)/shard_map/all_to_all | solution.py:316
  93.7 9.3 %copy-start.3 = (s32[128,6]{0,1:T(8,128)S(1)}, s32[128,6]{0,1:T(8,128)}, u32[]{:S(2)}) copy-start(s32[128,6]{0,1:T(8,128)} %param.25) | copy-start | bytes 9220
  98.0 82.3 %all-to-all-start.1 = ((bf16[16,144,768]{2,1,0:T(8,128)(2,1)}), bf16[16,144,768]{2,1,0:T(8,128)(2,1)}, u32[]{:S(2)}, u32[]{:S(2)}) async-start(bf16[16,144,768]{2,1,0:T(8,128)(2,1)} %ragged_attention.3), calls=%async_computation.1 | async-start | bytes 7077888 | tf_op jit(solution)/shard_map/all_to_all | solution.py:316
  103.0 93.4 %reduce-scatter.5.cloned.1.call-start = ((), (), s32[]{:S(2)}) async-start(), calls=%async_computation.10 | async-start | bytes 786432 | tf_op jit(solution)/shard_map/reduce_scatter | solution.py:322
  180.3 5.6 %copy-start.1 = (f32[128,2048]{1,0:T(8,128)S(1)}, f32[128,2048]{1,0:T(8,128)}, u32[]{:S(2)}) copy-start(f32[128,2048]{1,0:T(8,128)} %fusion.28) | copy-start | bytes 3145732
  185.9 10.5 %copy-start.2 = (bf16[128,1024]{1,0:T(8,128)(2,1)S(1)}, bf16[128,1024]{1,0:T(8,128)(2,1)}, u32[]{:S(2)}) copy-start(bf16[128,1024]{1,0:T(8,128)(2,1)} %param.15) | copy-start | bytes 786436
  202.6 32.8 %all-to-all-start.2 = ((bf16[16,32,1024]{2,1,0:T(8,128)(2,1)}), bf16[16,32,1024]{2,1,0:T(8,128)(2,1)}, u32[]{:S(2)}, u32[]{:S(2)}) async-start(bf16[16,32,1024]{2,1,0:T(8,128)(2,1)} %bitcast.84), calls=%async_computation.4 | async-start | bytes 2097152 | tf_op jit(solution)/shard_map/all_to_all | solution.py:371
  209.5 36.4 %all-gather.3.cloned.1.call-start = ((), (), s32[]{:S(2)}) async-start(), calls=%async_computation.12 | async-start | bytes 3145728 | tf_op jit(solution)/shard_map/all_gather | solution.py:386
  235.4 30.1 %all-to-all-start.3 = ((bf16[16,32,1024]{2,1,0:T(8,128)(2,1)}), bf16[16,32,1024]{2,1,0:T(8,128)(2,1)}, u32[]{:S(2)}, u32[]{:S(2)}) async-start(bf16[16,32,1024]{2,1,0:T(8,128)(2,1)} %bitcast.83), calls=%async_computation.5 | async-start | bytes 2097152 | tf_op jit(solution)/shard_map/all_to_all | solution.py:371
  241.0 34.4 %all-gather.5.cloned.1.call-start = ((), (), s32[]{:S(2)}) async-start(), calls=%async_computation.14 | async-start | bytes 3145728 | tf_op jit(solution)/shard_map/all_gather | solution.py:386
  265.6 22.9 %reduce-scatter.9.cloned.1.call-start = ((), (), s32[]{:S(2)}) async-start(), calls=%async_computation.13 | async-start | bytes 3145728 | tf_op jit(solution)/shard_map/reduce_scatter | solution.py:402
  271.8 49.4 %reduce-scatter.11.cloned.1.call-start = ((), (), s32[]{:S(2)}) async-start(), calls=%async_computation.15 | async-start | bytes 3145728 | tf_op jit(solution)/shard_map/reduce_scatter | solution.py:402
  286.4 40.0 %copy-start.4 = (bf16[1024,32]{0,1:T(8,128)(2,1)S(1)}, bf16[1024,32]{0,1:T(8,128)(2,1)}, u32[]{:S(2)}) copy-start(bf16[1024,32]{0,1:T(8,128)(2,1)} %param.24) | copy-start | bytes 196612
  321.1 29.8 %all-to-all-start.5 = ((bf16[16,32,1024]{2,1,0:T(8,128)(2,1)}), bf16[16,32,1024]{2,1,0:T(8,128)(2,1)}, u32[]{:S(2)}, u32[]{:S(2)}) async-start(bf16[16,32,1024]{2,1,0:T(8,128)(2,1)} %bitcast.85), calls=%async_computation.9 | async-start | bytes 2097152 | tf_op jit(solution)/shard_map/all_to_all | solution.py:405
  326.4 28.4 %reduce-scatter.7.cloned.1.call-start = ((), (), s32[]{:S(2)}) async-start(), calls=%async_computation.11 | async-start | bytes 786432 | tf_op jit(solution)/shard_map/reduce_scatter | solution.py:342
Sparse Core Ops, SparseCore 0:
  189.4 7.0 reduce-scatter.4
  235.5 10.3 all-gather.2
  265.7 9.6 all-gather.4
  277.6 10.7 reduce-scatter.8
  290.5 10.7 reduce-scatter.10
  337.3 9.1 reduce-scatter.6
